TPU v7x, 256 devices: a whole 4x4x8 slice. The times are simulated.
256 devices in a mesh: dp: 8 (over y, core), tm: 32 (over z, x).
Axes of the slice: x: 4, y: 4, z: 8, core: 2. Of those that a mesh axis runs over, the one named last changes fastest.
Arguments:
- grad_attn: bfloat16 [8, 8192, 1024], P('dp', 'tm'), may hold values from -6 to 6
- route: int32 [8, 8192], P('dp', 'tm'), may hold values from 0 to 8191, as said below
- lengths: int32 [8, 4], P('dp'), may hold values from 1 to 4096, 8192 in all within a row
- conv_pre: bfloat16 [8, 8192, 512], P('dp', 'tm'), may hold values from -6 to 6
- conv_in: bfloat16 [8, 16384, 512], P('dp', 'tm'), may hold values from -6 to 6
- conv_w: bfloat16 [3, 512, 512], replicated, may hold values from -0.15625 to 0.15625
- proj_w: bfloat16 [512, 1024], replicated, may hold values from -0.25 to 0.25
- in_w: bfloat16 [1024, 2048], replicated, may hold values from -0.1875 to 0.1875
- depth_w: bfloat16 [31, 1024], replicated, may hold values from -1 to 1
- depth_gain: bfloat16 [1024], replicated, may hold values from 0.099609375 to 1.8984375
- out_w: bfloat16 [1024, 1024], replicated, may hold values from -0.1875 to 0.1875
Outputs:
- input_grad: float32 [8, 16384, 512], P('dp', 'tm')
- conv_grad: float32 [3, 512, 512], P(None, 'tm')
- proj_grad: float32 [512, 1024], P('tm')
- in_grad: float32 [1024, 2048], P('tm')
- depth_grad: float32 [31, 1024], P(None, 'tm')
- gain_grad: float32 [1024], P('tm')
- out_grad: float32 [1024, 1024], P('tm')
Inputs may be any that keep to these rules, and one draw needn't show every extreme that they name: `route`: each row is a permutation of the frames. Of the 256 attention positions on one device, at most 16 hold frames of any one block of 256 consecutive frames, and every block takes at most 16 from one device's positions; in every packed batch this bound is reached. `lengths`: each row sums to 8192.
All inputs are finite; a program needn't handle non-finite values.
Results may differ from a plain program's by a relative error of at most 0.009.
Values may be sent and summed in bfloat16 or wider, within the bound.
A program may use at most 128 MiB of HBM per device.

v0:
```python
import math

import jax
import jax.numpy as jnp
from jax import lax
from jax.sharding import PartitionSpec as P

epsilon = 1e-05


def extended(cells, sides, width):
    for axis, dim in sides:
        count = lax.axis_size(axis)
        ends = count - 1
        head = lax.slice_in_dim(cells, 0, width, axis=dim)
        tail = lax.slice_in_dim(cells, cells.shape[dim] - width, cells.shape[dim], axis=dim)
        cells = jnp.concatenate(
            [
                lax.ppermute(tail, axis, [(i, (i + 1) % count) for i in range(ends)]),
                cells,
                lax.ppermute(head, axis, [((i + 1) % count, i) for i in range(ends)]),
            ],
            axis=dim,
        )
    return cells


def passed_along(block, axis, distance):
    devices = range(lax.axis_size(axis))
    route = [(i - distance, i) for i in devices if i - distance in devices]
    return lax.ppermute(block, axis, route)


def gelu_exact(value):
    return 0.5 * value * (1.0 + jax.scipy.special.erf(value / math.sqrt(2.0)))


def gelu_slope(value):
    return 0.5 * (1.0 + jax.scipy.special.erf(value / math.sqrt(2.0))) + value * jnp.exp(
        -0.5 * value * value
    ) / math.sqrt(2.0 * math.pi)


def segment_of(lengths_row, positions):
    bounds = jnp.cumsum(lengths_row)
    return jnp.sum((positions[:, None] >= bounds[None, :]).astype(jnp.int32), axis=1)


def gated(joined, width):
    linear = joined[:, :width]
    sigma = jax.nn.sigmoid(joined[:, width:])
    return (linear, sigma, (linear * sigma).astype(jnp.bfloat16))


def per_device(
    grad_attn, route, lengths, conv_pre, conv_in, conv_w, proj_w, in_w, depth_w, depth_gain, out_w
):
    rows_grad = grad_attn[0]
    order = route[0]
    lengths_row = lengths[0]
    pre_rows = conv_pre[0]
    in_rows = conv_in[0]
    frames = rows_grad.shape[0]
    width = rows_grad.shape[1]
    channels = proj_w.shape[0]
    kernel = depth_w.shape[0]
    half = (kernel - 1) // 2
    owners = lax.axis_size("tm")
    mine_index = lax.axis_index("tm")
    capacity = 2 * frames // owners
    owner_of = order // frames
    owner_hot = (owner_of[:, None] == jnp.arange(owners, dtype=jnp.int32)[None, :]).astype(
        jnp.int32
    )
    send_rank = jnp.sum((jnp.cumsum(owner_hot, axis=0) - owner_hot) * owner_hot, axis=1)
    send_slot = owner_of * capacity + send_rank
    outgoing = jnp.zeros((owners * capacity, width), jnp.bfloat16).at[send_slot].set(rows_grad)
    incoming = lax.all_to_all(outgoing, "tm", split_axis=0, concat_axis=0, tiled=True)
    all_orders = lax.all_gather(order, "tm", axis=0, tiled=True).reshape(owners, frames)
    is_mine = (all_orders // frames == mine_index).astype(jnp.int32)
    recv_rank = jnp.cumsum(is_mine, axis=1) - is_mine
    recv_slot = jnp.arange(owners, dtype=jnp.int32)[:, None] * capacity + recv_rank
    target = jnp.where(is_mine > 0, all_orders - mine_index * frames, frames)
    slot_of_frame = (
        jnp.zeros((frames,), jnp.int32)
        .at[target.reshape(-1)]
        .set(recv_slot.reshape(-1), mode="drop")
    )
    upstream = incoming[slot_of_frame]
    total_frames = frames * owners
    positions = mine_index * frames + jnp.arange(frames, dtype=jnp.int32)
    segment = segment_of(lengths_row, positions)
    wide_pos = mine_index * frames - half + jnp.arange(frames + 2 * half, dtype=jnp.int32)
    inside = (wide_pos >= 0) & (wide_pos < total_frames)
    wide_seg = jnp.where(inside, segment_of(lengths_row, wide_pos), -1)
    activ = gelu_exact(pre_rows.astype(jnp.float32)).astype(jnp.bfloat16)
    features = jnp.dot(activ, proj_w, preferred_element_type=jnp.float32).astype(jnp.bfloat16)
    linear, sigma, glu_out = gated(
        jnp.dot(features, in_w, preferred_element_type=jnp.float32), width
    )
    glu_wide = extended(glu_out, (("tm", 0),), half)
    taps = depth_w.astype(jnp.float32)
    mixed = jnp.zeros((frames, width), jnp.float32)
    for offset in range(kernel):
        linked = (wide_seg[offset : offset + frames] == segment).astype(jnp.float32)[:, None]
        mixed = (
            mixed + taps[offset] * glu_wide[offset : offset + frames].astype(jnp.float32) * linked
        )
    center = jnp.mean(mixed, axis=1, keepdims=True)
    spread = jnp.mean((mixed - center) ** 2, axis=1, keepdims=True)
    inv_std = 1.0 / jnp.sqrt(spread + epsilon)
    normed = (mixed - center) * inv_std
    gain = depth_gain.astype(jnp.float32)
    scaled = normed * gain
    sig_scaled = jax.nn.sigmoid(scaled)
    swished = (scaled * sig_scaled).astype(jnp.bfloat16)
    out_term = jnp.dot(swished.T, upstream, preferred_element_type=jnp.float32)
    dswish = jnp.dot(upstream, out_w.T, preferred_element_type=jnp.float32)
    dscaled = dswish * sig_scaled * (1.0 + scaled * (1.0 - sig_scaled))
    gain_term = jnp.sum(dscaled * normed, axis=0)
    qterm = dscaled * gain
    dmixed_f = inv_std * (
        qterm
        - jnp.mean(qterm, axis=1, keepdims=True)
        - normed * jnp.mean(qterm * normed, axis=1, keepdims=True)
    )
    dmixed_wide = extended(dmixed_f, (("tm", 0),), half)
    dglu = jnp.zeros((frames, width), jnp.float32)
    depth_rows = []
    for offset in range(kernel):
        linked = (wide_seg[offset : offset + frames] == segment).astype(jnp.float32)[:, None]
        depth_rows.append(
            jnp.sum(
                glu_wide[offset : offset + frames].astype(jnp.float32) * dmixed_f * linked, axis=0
            )
        )
        start = 2 * half - offset
        linked_back = (wide_seg[start : start + frames] == segment).astype(jnp.float32)[:, None]
        dglu = dglu + taps[offset] * dmixed_wide[start : start + frames] * linked_back
    depth_term = jnp.stack(depth_rows, axis=0)
    djoined = jnp.concatenate([dglu * sigma, dglu * linear * sigma * (1.0 - sigma)], axis=1).astype(
        jnp.bfloat16
    )
    in_term = jnp.dot(features.T, djoined, preferred_element_type=jnp.float32)
    dfeatures = (
        upstream.astype(jnp.float32) + jnp.dot(djoined, in_w.T, preferred_element_type=jnp.float32)
    ).astype(jnp.bfloat16)
    proj_term = jnp.dot(activ.T, dfeatures, preferred_element_type=jnp.float32)
    dpre = (
        jnp.dot(dfeatures, proj_w.T, preferred_element_type=jnp.float32)
        * gelu_slope(pre_rows.astype(jnp.float32))
    ).astype(jnp.bfloat16)
    next_first = passed_along(dpre[:1], "tm", -1)
    dpre_next = jnp.concatenate([dpre[1:], next_first], axis=0)
    paired = in_rows.reshape(frames, 2, channels)
    even_rows = paired[:, 0]
    odd_rows = paired[:, 1]
    grad_even = jnp.dot(dpre, conv_w[1].T, preferred_element_type=jnp.float32)
    grad_odd = jnp.dot(dpre, conv_w[2].T, preferred_element_type=jnp.float32) + jnp.dot(
        dpre_next, conv_w[0].T, preferred_element_type=jnp.float32
    )
    input_rows = jnp.stack([grad_even, grad_odd], axis=1).reshape(2 * frames, channels)
    conv_term = jnp.stack(
        [
            jnp.dot(odd_rows.T, dpre_next, preferred_element_type=jnp.float32),
            jnp.dot(even_rows.T, dpre, preferred_element_type=jnp.float32),
            jnp.dot(odd_rows.T, dpre, preferred_element_type=jnp.float32),
        ],
        axis=0,
    )
    summed = (
        lax.psum_scatter(conv_term, "tm", scatter_dimension=1, tiled=True),
        lax.psum_scatter(proj_term, "tm", scatter_dimension=0, tiled=True),
        lax.psum_scatter(in_term, "tm", scatter_dimension=0, tiled=True),
        lax.psum_scatter(depth_term, "tm", scatter_dimension=1, tiled=True),
        lax.psum_scatter(gain_term, "tm", scatter_dimension=0, tiled=True),
        lax.psum_scatter(out_term, "tm", scatter_dimension=0, tiled=True),
    )
    conv_sum, proj_sum, in_sum, depth_sum, gain_sum, out_sum = lax.psum(
        (summed[0], summed[1], summed[2], summed[3], summed[4], summed[5]), "dp"
    )
    factor = 1.0 / math.sqrt(total_frames * lax.axis_size("dp"))
    return (
        input_rows[None],
        conv_sum * factor,
        proj_sum * factor,
        in_sum * factor,
        depth_sum * factor,
        gain_sum * factor,
        out_sum * factor,
    )


def solution(mesh):
    placed = (
        P("dp", "tm", None),
        P("dp", "tm"),
        P("dp", None),
        P("dp", "tm", None),
        P("dp", "tm", None),
        P(),
        P(),
        P(),
        P(),
        P(),
        P(),
    )
    return jax.shard_map(
        per_device,
        mesh=mesh,
        in_specs=placed,
        out_specs=(
            P("dp", "tm", None),
            P(None, "tm", None),
            P("tm", None),
            P("tm", None),
            P(None, "tm"),
            P("tm"),
            P("tm", None),
        ),
        check_vma=False,
    )
```

profile of v0, /device:TPU:1, one launch (start us, length us, event | category | flops | bytes accessed | tf_op | source)
XLA Modules:
  0.0 1311.6 jit_solution(3411893817151026160)
XLA Ops:
  7.2 1.9 convolution_convert_fusion
  9.1 3.6 fusion.337
  12.8 1.3 copy-done.3
  14.5 4.1 collective-permute-start
  18.5 1.3 collective-permute-start.1
  19.9 0.6 reduce-window.21
  20.8 2.6 scatter_custom_fusion
  23.5 12.9 all-to-all-start
  36.9 0.7 compare_convert_fusion.29
  37.6 0.6 compare_convert_fusion.28
  38.7 47.6 %all-gather = s32[1,8192]{1,0:T(1,128)S(1)} all-gather(s32[1,256]{1,0:T(1,128)S(1)} %copy-done.50), channel_id=2, replica_groups=mesh['dp'=8,'tm'=32] {'tm'}, dimensions={1}, use_global_device_ids=true | all-gather | bytes 33792 | tf_op jit(solution)/shard_map/all_gather | solution.py:79
  86.4 0.6 reduce-window.30
  87.5 30.6 %scatter_custom_fusion.1 = s32[256]{0:T(256)S(1)} fusion(s32[8192]{0:T(1024)S(1)} %get-tuple-element.125, s32[8192]{0:T(1024)S(1)} %get-tuple-element.124, s32[]{:T(128)} %constant.33.clone.1), kind=kCustom, calls=%fused_computation.580 | custom fusion | bytes 1028 | tf_op jit(solution)/shard_map/scatter | solution.py:87
  118.1 1.2 reshape_squeeze.3
  119.3 1.8 fusion.333
  121.1 0.6 convert_element_type.410
  121.8 10.2 fusion.330
  132.3 1.0 copy-done.5
  133.6 3.8 gather_fusion
  137.4 3.0 multiply_reduce_fusion
  140.5 4.2 fusion.126
  144.7 1.3 collective-permute-start.2
  146.0 4.2 collective-permute-start.3
  150.3 4.5 fusion.123
  154.8 2.8 fusion.72
  157.6 2.3 fusion.54
  159.9 2.0 fusion.84
  161.9 1.9 fusion.36
  163.8 3.1 stack.155
  166.9 1.0 copy.57
  168.1 10.4 multiply_convert_fusion.2
  179.0 0.8 copy-done.18
  179.7 1.3 fusion.1
  181.7 1.3 collective-permute-start.4
  183.7 2.3 collective-permute-done.4
  186.3 2.0 pad_maximum_fusion
  188.3 5.2 copy.55
  193.8 2.9 fusion.324
  196.9 3.9 fusion.249
  200.9 1.0 copy-done.12
  202.0 5.6 fusion.248
  207.7 0.6 copy-done.82
  208.3 0.6 dynamic-slice
  210.1 58.7 %all-reduce.1 = f32[1024]{0:T(1024)S(1)} all-reduce(f32[1024]{0:T(1024)S(1)} %copy-done.75), channel_id=7, replica_groups=mesh['dp'=8,'tm'=32] {'tm'}, use_global_device_ids=true, to_apply=%region_54.55.clone | all-reduce | flops 1024 | bytes 8192
  269.0 1.4 convolution_bitcast_fusion.3
  270.3 1.4 fusion.286
  271.7 1.4 fusion.2
  273.2 0.8 copy.54
  274.0 1.7 broadcast_in_dim_reshape.3
  275.7 112.4 %reduce-scatter.13.cloned.1.call-done = f32[32,31]{1,0:T(8,128)} async-done(((f32[1024,31]{1,0:T(8,128)}), f32[32,31]{1,0:T(8,128)}) %reduce-scatter.13.cloned.1.call-update) | async-done | bytes 3984
  388.1 0.8 copy.58
  388.9 26.5 %all-reduce.2 = (f32[31,32]{1,0:T(8,128)S(1)}, f32[32]{0:T(128)S(1)}) all-reduce(f32[31,32]{1,0:T(8,128)S(1)} %copy.58, f32[32]{0:T(128)S(1)} %dynamic-slice.3), channel_id=1, replica_groups=mesh['dp'=8,'tm'=32] {'dp'}, use_global_device_ids=true, to_apply=%region_52.53 | all-reduce | flops 1024 | bytes 8192 | tf_op jit(solution)/shard_map/psum | solution.py:179
  415.5 141.9 %all-reduce.7.cloned.1.call-done = f32[3,512,512]{2,0,1:T(4,128)} async-done(((f32[3,512,512]{2,0,1:T(4,128)}), f32[3,512,512]{2,0,1:T(4,128)}) %all-reduce.7.cloned.1.call-update) | async-done | bytes 3145744
  557.3 1.6 constant_dynamic-slice_fusion
  558.9 213.4 %reduce-scatter.7.cloned.1.call-done = f32[16,1024]{1,0:T(8,128)} async-done(((f32[512,1024]{1,0:T(8,128)}), f32[16,1024]{1,0:T(8,128)}) %reduce-scatter.7.cloned.1.call-update) | async-done | bytes 65552 | tf_op jit(solution)/shard_map/reduce_scatter | solution.py:173
  772.3 224.2 %reduce-scatter.11.cloned.1.call-done = f32[32,1024]{1,0:T(8,128)} async-done(((f32[1024,1024]{1,0:T(8,128)}), f32[32,1024]{1,0:T(8,128)}) %reduce-scatter.11.cloned.1.call-update) | async-done | bytes 131088 | tf_op jit(solution)/shard_map/reduce_scatter | solution.py:177
  996.5 231.9 %reduce-scatter.9.cloned.1.call-done = f32[32,2048]{1,0:T(8,128)} async-done(((f32[1024,2048]{1,0:T(8,128)}), f32[32,2048]{1,0:T(8,128)}) %reduce-scatter.9.cloned.1.call-update) | async-done | bytes 262160 | tf_op jit(solution)/shard_map/reduce_scatter | solution.py:174
  1229.0 0.6 broadcast_multiply_fusion.4
  1229.6 68.8 %all-reduce.9.cloned.1.call-done = (f32[3,16,512]{2,0,1:T(4,128)}, f32[16,1024]{1,0:T(8,128)}, f32[32,2048]{1,0:T(8,128)}, f32[32,1024]{1,0:T(8,128)}) async-done(((f32[3,16,512]{2,0,1:T(4,128)}, f32[16,1024]{1,0:T(8,128)}, f32[32,2048]{1,0:T(8,128)}, f32[32,1024]{1,0:T(8,128)}), (f32[3,16,512]{2,0,1:T(4,128)}, f32[16,1024]{1,0:T(8,128)}, f32[32,2048]{1,0:T(8,128)}, ...) | async-done | bytes 557072 | tf_op jit(solution)/shard_map/psum | solution.py:179
  1298.4 1.7 broadcast_multiply_fusion
  1300.1 0.9 broadcast_multiply_fusion.2
  1301.0 0.7 copy.56
  1301.7 1.6 broadcast_multiply_fusion.1
  1303.2 1.5 broadcast_multiply_fusion.3
  (223 shorter events, 5.7 us)
Async XLA Ops:
  7.2 130.2 %copy-start = (bf16[1024,1024]{1,0:T(8,128)(2,1)S(1)}, bf16[1024,1024]{1,0:T(8,128)(2,1)}, u32[]{:S(2)}) copy-start(bf16[1024,1024]{1,0:T(8,128)(2,1)} %param.21) | copy-start | bytes 6291460
  14.4 107.3 %copy-start.1 = (bf16[256,1024]{1,0:T(8,128)(2,1)}, bf16[256,1024]{1,0:T(8,128)(2,1)S(1)}, u32[]{:S(2)}) copy-start(bf16[256,1024]{1,0:T(8,128)(2,1)S(1)} %multiply_convert_fusion.3) | copy-start | bytes 1572868
  14.4 22.1 %copy-start.81 = (s32[1,4]{1,0:T(1,128)S(1)}, s32[1,4]{1,0:T(1,128)}, u32[]{:S(2)}) copy-start(s32[1,4]{1,0:T(1,128)} %param.13) | copy-start | bytes 52
  14.4 23.8 %copy-start.22 = (bf16[31,1024]{1,0:T(8,128)(2,1)S(1)}, bf16[31,1024]{1,0:T(8,128)(2,1)}, u32[]{:S(2)}) copy-start(bf16[31,1024]{1,0:T(8,128)(2,1)} %param.19) | copy-start | bytes 190468
  14.5 107.3 %collective-permute-start = (bf16[15,1024]{1,0:T(8,128)(2,1)S(1)}, bf16[15,1024]{1,0:T(8,128)(2,1)S(1)}, u32[]{:S(2)}, u32[]{:S(2)}) collective-permute-start(bf16[15,1024]{1,0:T(8,128)(2,1)S(1)} %get-tuple-element.91), channel_id=1, source_target_pairs={{0,1},{1,2},{2,3},{3,4},{4,5},{5,6},{6,7},{7,8},{8,9},{9,10},{10,1... | collective-permute-start | bytes 92168 | tf_op jit(solution)/shard_map/ppermute | solution.py:19
  18.5 103.2 %collective-permute-start.1 = (bf16[15,1024]{1,0:T(8,128)(2,1)S(1)}, bf16[15,1024]{1,0:T(8,128)(2,1)S(1)}, u32[]{:S(2)}, u32[]{:S(2)}) collective-permute-start(bf16[15,1024]{1,0:T(8,128)(2,1)S(1)} %get-tuple-element.92), channel_id=1, source_target_pairs={{1,0},{2,1},{3,2},{4,3},{5,4},{6,5},{7,6},{8,7},{9,8},{10,9},{11,1... | collective-permute-start | bytes 92168 | tf_op jit(solution)/shard_map/ppermute | solution.py:21
  23.5 110.1 %all-to-all-start = ((bf16[32,16,1024]{2,1,0:T(8,128)(2,1)}), bf16[32,16,1024]{2,1,0:T(8,128)(2,1)}, u32[]{:S(2)}, u32[]{:S(2)}) async-start(bf16[32,16,1024]{2,1,0:T(8,128)(2,1)} %bitcast.174), calls=%async_computation | async-start | bytes 2097152 | tf_op jit(solution)/shard_map/all_to_all | solution.py:78
  36.4 84.7 %copy-start.78 = (bf16[1024]{0:T(1024)(128)(2,1)S(1)}, bf16[1024]{0:T(1024)(128)(2,1)}, u32[]{:S(2)}) copy-start(bf16[1024]{0:T(1024)(128)(2,1)} %param.20) | copy-start | bytes 6148
  36.4 351.7 %reduce-scatter.13.cloned.1.call-start = ((), (), s32[]{:S(2)}) async-start(), calls=%async_computation.8 | async-start | bytes 540672
  38.2 83.5 %copy-start.51 = (f32[256]{0:T(256)}, f32[256]{0:T(256)S(1)}, u32[]{:S(2)}) copy-start(f32[256]{0:T(256)S(1)} %get-tuple-element.145) | copy-start | bytes 3076
  38.2 83.5 %copy-start.53 = (f32[256]{0:T(256)}, f32[256]{0:T(256)S(1)}, u32[]{:S(2)}) copy-start(f32[256]{0:T(256)S(1)} %get-tuple-element.146) | copy-start | bytes 3076
  38.3 83.5 %copy-start.55 = (f32[256]{0:T(256)}, f32[256]{0:T(256)S(1)}, u32[]{:S(2)}) copy-start(f32[256]{0:T(256)S(1)} %get-tuple-element.147) | copy-start | bytes 3076
  38.3 83.5 %copy-start.57 = (f32[256]{0:T(256)}, f32[256]{0:T(256)S(1)}, u32[]{:S(2)}) copy-start(f32[256]{0:T(256)S(1)} %get-tuple-element.148) | copy-start | bytes 3076
  38.3 83.5 %copy-start.59 = (f32[256]{0:T(256)}, f32[256]{0:T(256)S(1)}, u32[]{:S(2)}) copy-start(f32[256]{0:T(256)S(1)} %get-tuple-element.149) | copy-start | bytes 3076
  38.3 83.5 %copy-start.61 = (f32[256]{0:T(256)}, f32[256]{0:T(256)S(1)}, u32[]{:S(2)}) copy-start(f32[256]{0:T(256)S(1)} %get-tuple-element.150) | copy-start | bytes 3076
  38.3 83.5 %copy-start.63 = (f32[256]{0:T(256)}, f32[256]{0:T(256)S(1)}, u32[]{:S(2)}) copy-start(f32[256]{0:T(256)S(1)} %get-tuple-element.151) | copy-start | bytes 3076
  38.3 83.5 %copy-start.65 = (f32[256]{0:T(256)}, f32[256]{0:T(256)S(1)}, u32[]{:S(2)}) copy-start(f32[256]{0:T(256)S(1)} %get-tuple-element.152) | copy-start | bytes 3076
  38.3 83.5 %copy-start.67 = (f32[256]{0:T(256)}, f32[256]{0:T(256)S(1)}, u32[]{:S(2)}) copy-start(f32[256]{0:T(256)S(1)} %get-tuple-element.153) | copy-start | bytes 3076
  38.3 83.5 %copy-start.69 = (f32[256]{0:T(256)}, f32[256]{0:T(256)S(1)}, u32[]{:S(2)}) copy-start(f32[256]{0:T(256)S(1)} %get-tuple-element.154) | copy-start | bytes 3076
  38.3 83.5 %copy-start.71 = (f32[256]{0:T(256)}, f32[256]{0:T(256)S(1)}, u32[]{:S(2)}) copy-start(f32[256]{0:T(256)S(1)} %get-tuple-element.155) | copy-start | bytes 3076
  38.4 93.6 %copy-start.23 = (f32[1,1024]{1,0:T(1,128)}, f32[1,1024]{1,0:T(1,128)S(1)}, u32[]{:S(2)}) copy-start(f32[1,1024]{1,0:T(1,128)S(1)} %get-tuple-element.97) | copy-start | bytes 12292
  38.4 93.6 %copy-start.24 = (f32[1,1024]{1,0:T(1,128)}, f32[1,1024]{1,0:T(1,128)S(1)}, u32[]{:S(2)}) copy-start(f32[1,1024]{1,0:T(1,128)S(1)} %get-tuple-element.98) | copy-start | bytes 12292
  38.4 93.6 %copy-start.25 = (f32[1,1024]{1,0:T(1,128)}, f32[1,1024]{1,0:T(1,128)S(1)}, u32[]{:S(2)}) copy-start(f32[1,1024]{1,0:T(1,128)S(1)} %get-tuple-element.99) | copy-start | bytes 12292
  38.4 93.6 %copy-start.26 = (f32[1,1024]{1,0:T(1,128)}, f32[1,1024]{1,0:T(1,128)S(1)}, u32[]{:S(2)}) copy-start(f32[1,1024]{1,0:T(1,128)S(1)} %get-tuple-element.100) | copy-start | bytes 12292
  38.4 93.6 %copy-start.27 = (f32[1,1024]{1,0:T(1,128)}, f32[1,1024]{1,0:T(1,128)S(1)}, u32[]{:S(2)}) copy-start(f32[1,1024]{1,0:T(1,128)S(1)} %get-tuple-element.101) | copy-start | bytes 12292
  38.5 93.6 %copy-start.28 = (f32[1,1024]{1,0:T(1,128)}, f32[1,1024]{1,0:T(1,128)S(1)}, u32[]{:S(2)}) copy-start(f32[1,1024]{1,0:T(1,128)S(1)} %get-tuple-element.102) | copy-start | bytes 12292
  38.5 93.6 %copy-start.29 = (f32[1,1024]{1,0:T(1,128)}, f32[1,1024]{1,0:T(1,128)S(1)}, u32[]{:S(2)}) copy-start(f32[1,1024]{1,0:T(1,128)S(1)} %get-tuple-element.103) | copy-start | bytes 12292
  38.5 93.6 %copy-start.30 = (f32[1,1024]{1,0:T(1,128)}, f32[1,1024]{1,0:T(1,128)S(1)}, u32[]{:S(2)}) copy-start(f32[1,1024]{1,0:T(1,128)S(1)} %get-tuple-element.104) | copy-start | bytes 12292
  38.5 93.6 %copy-start.31 = (f32[1,1024]{1,0:T(1,128)}, f32[1,1024]{1,0:T(1,128)S(1)}, u32[]{:S(2)}) copy-start(f32[1,1024]{1,0:T(1,128)S(1)} %get-tuple-element.105) | copy-start | bytes 12292
  38.5 93.6 %copy-start.32 = (f32[1,1024]{1,0:T(1,128)}, f32[1,1024]{1,0:T(1,128)S(1)}, u32[]{:S(2)}) copy-start(f32[1,1024]{1,0:T(1,128)S(1)} %get-tuple-element.106) | copy-start | bytes 12292
  38.5 93.6 %copy-start.33 = (f32[1,1024]{1,0:T(1,128)}, f32[1,1024]{1,0:T(1,128)S(1)}, u32[]{:S(2)}) copy-start(f32[1,1024]{1,0:T(1,128)S(1)} %get-tuple-element.107) | copy-start | bytes 12292
  38.5 93.6 %copy-start.34 = (f32[1,1024]{1,0:T(1,128)}, f32[1,1024]{1,0:T(1,128)S(1)}, u32[]{:S(2)}) copy-start(f32[1,1024]{1,0:T(1,128)S(1)} %get-tuple-element.108) | copy-start | bytes 12292
  38.5 93.6 %copy-start.35 = (f32[1,1024]{1,0:T(1,128)}, f32[1,1024]{1,0:T(1,128)S(1)}, u32[]{:S(2)}) copy-start(f32[1,1024]{1,0:T(1,128)S(1)} %get-tuple-element.109) | copy-start | bytes 12292
  38.5 93.6 %copy-start.36 = (f32[1,1024]{1,0:T(1,128)}, f32[1,1024]{1,0:T(1,128)S(1)}, u32[]{:S(2)}) copy-start(f32[1,1024]{1,0:T(1,128)S(1)} %get-tuple-element.110) | copy-start | bytes 12292
  38.5 93.6 %copy-start.37 = (f32[1,1024]{1,0:T(1,128)}, f32[1,1024]{1,0:T(1,128)S(1)}, u32[]{:S(2)}) copy-start(f32[1,1024]{1,0:T(1,128)S(1)} %get-tuple-element.111) | copy-start | bytes 12292
  38.6 93.6 %copy-start.38 = (f32[1,1024]{1,0:T(1,128)}, f32[1,1024]{1,0:T(1,128)S(1)}, u32[]{:S(2)}) copy-start(f32[1,1024]{1,0:T(1,128)S(1)} %get-tuple-element.112) | copy-start | bytes 12292
  38.6 93.6 %copy-start.39 = (f32[1,1024]{1,0:T(1,128)}, f32[1,1024]{1,0:T(1,128)S(1)}, u32[]{:S(2)}) copy-start(f32[1,1024]{1,0:T(1,128)S(1)} %get-tuple-element.113) | copy-start | bytes 12292
  38.6 93.6 %copy-start.40 = (f32[1,1024]{1,0:T(1,128)}, f32[1,1024]{1,0:T(1,128)S(1)}, u32[]{:S(2)}) copy-start(f32[1,1024]{1,0:T(1,128)S(1)} %get-tuple-element.114) | copy-start | bytes 12292
  38.6 93.6 %copy-start.41 = (f32[1,1024]{1,0:T(1,128)}, f32[1,1024]{1,0:T(1,128)S(1)}, u32[]{:S(2)}) copy-start(f32[1,1024]{1,0:T(1,128)S(1)} %get-tuple-element.115) | copy-start | bytes 12292
  38.6 93.6 %copy-start.42 = (f32[1,1024]{1,0:T(1,128)}, f32[1,1024]{1,0:T(1,128)S(1)}, u32[]{:S(2)}) copy-start(f32[1,1024]{1,0:T(1,128)S(1)} %get-tuple-element.116) | copy-start | bytes 12292
  38.7 93.6 %copy-start.43 = (f32[1,1024]{1,0:T(1,128)}, f32[1,1024]{1,0:T(1,128)S(1)}, u32[]{:S(2)}) copy-start(f32[1,1024]{1,0:T(1,128)S(1)} %get-tuple-element.117) | copy-start | bytes 12292
  38.7 93.6 %copy-start.44 = (f32[1,1024]{1,0:T(1,128)}, f32[1,1024]{1,0:T(1,128)S(1)}, u32[]{:S(2)}) copy-start(f32[1,1024]{1,0:T(1,128)S(1)} %get-tuple-element.118) | copy-start | bytes 12292
  38.7 93.6 %copy-start.45 = (f32[1,1024]{1,0:T(1,128)}, f32[1,1024]{1,0:T(1,128)S(1)}, u32[]{:S(2)}) copy-start(f32[1,1024]{1,0:T(1,128)S(1)} %get-tuple-element.119) | copy-start | bytes 12292
  38.7 93.6 %copy-start.46 = (f32[1,1024]{1,0:T(1,128)}, f32[1,1024]{1,0:T(1,128)S(1)}, u32[]{:S(2)}) copy-start(f32[1,1024]{1,0:T(1,128)S(1)} %get-tuple-element.120) | copy-start | bytes 12292
  38.7 93.6 %copy-start.47 = (f32[1,1024]{1,0:T(1,128)}, f32[1,1024]{1,0:T(1,128)S(1)}, u32[]{:S(2)}) copy-start(f32[1,1024]{1,0:T(1,128)S(1)} %get-tuple-element.121) | copy-start | bytes 12292
  38.7 93.6 %copy-start.48 = (f32[1,1024]{1,0:T(1,128)}, f32[1,1024]{1,0:T(1,128)S(1)}, u32[]{:S(2)}) copy-start(f32[1,1024]{1,0:T(1,128)S(1)} %get-tuple-element.122) | copy-start | bytes 12292
  38.7 93.6 %copy-start.49 = (f32[1,1024]{1,0:T(1,128)}, f32[1,1024]{1,0:T(1,128)S(1)}, u32[]{:S(2)}) copy-start(f32[1,1024]{1,0:T(1,128)S(1)} %get-tuple-element.123) | copy-start | bytes 12292
  140.4 14.4 %copy-start.52 = (f32[256]{0:T(256)S(1)}, f32[256]{0:T(256)}, u32[]{:S(2)}) copy-start(f32[256]{0:T(256)} %copy-done.51) | copy-start | bytes 3076
  140.4 14.4 %copy-start.54 = (f32[256]{0:T(256)S(1)}, f32[256]{0:T(256)}, u32[]{:S(2)}) copy-start(f32[256]{0:T(256)} %copy-done.53) | copy-start | bytes 3076
  140.5 14.4 %copy-start.56 = (f32[256]{0:T(256)S(1)}, f32[256]{0:T(256)}, u32[]{:S(2)}) copy-start(f32[256]{0:T(256)} %copy-done.55) | copy-start | bytes 3076
  140.5 14.3 %copy-start.58 = (f32[256]{0:T(256)S(1)}, f32[256]{0:T(256)}, u32[]{:S(2)}) copy-start(f32[256]{0:T(256)} %copy-done.57) | copy-start | bytes 3076
  140.5 14.3 %copy-start.60 = (f32[256]{0:T(256)S(1)}, f32[256]{0:T(256)}, u32[]{:S(2)}) copy-start(f32[256]{0:T(256)} %copy-done.59) | copy-start | bytes 3076
  144.7 12.9 copy-start.68
  144.7 12.9 copy-start.70
  144.7 12.9 copy-start.72
  144.7 23.3 %collective-permute-start.2 = (f32[15,1024]{1,0:T(8,128)S(1)}, f32[15,1024]{1,0:T(8,128)S(1)}, u32[]{:S(2)}, u32[]{:S(2)}) collective-permute-start(f32[15,1024]{1,0:T(8,128)S(1)} %get-tuple-element.87), channel_id=1, source_target_pairs={{1,0},{2,1},{3,2},{4,3},{5,4},{6,5},{7,6},{8,7},{9,8},{10,9},{11,1... | collective-permute-start | bytes 184328 | tf_op jit(solution)/shard_map/ppermute | solution.py:21
  146.0 22.0 %collective-permute-start.3 = (f32[15,1024]{1,0:T(8,128)S(1)}, f32[15,1024]{1,0:T(8,128)S(1)}, u32[]{:S(2)}, u32[]{:S(2)}) collective-permute-start(f32[15,1024]{1,0:T(8,128)S(1)} %get-tuple-element.88), channel_id=1, source_target_pairs={{0,1},{1,2},{2,3},{3,4},{4,5},{5,6},{6,7},{7,8},{8,9},{9,10},{10,1... | collective-permute-start | bytes 184328 | tf_op jit(solution)/shard_map/ppermute | solution.py:19
  168.0 389.3 %all-reduce.7.cloned.1.call-start = ((), (), s32[]{:S(2)}) async-start(), calls=%async_computation.9 | async-start | bytes 8388608
  181.7 4.3 collective-permute-start.4
  193.5 578.8 %reduce-scatter.7.cloned.1.call-start = ((), (), s32[]{:S(2)}) async-start(), calls=%async_computation.5 | async-start | bytes 2162688 | tf_op jit(solution)/shard_map/reduce_scatter | solution.py:173
  196.8 799.7 %reduce-scatter.11.cloned.1.call-start = ((), (), s32[]{:S(2)}) async-start(), calls=%async_computation.7 | async-start | bytes 4325376 | tf_op jit(solution)/shard_map/reduce_scatter | solution.py:177
  200.8 1027.6 %reduce-scatter.9.cloned.1.call-start = ((), (), s32[]{:S(2)}) async-start(), calls=%async_computation.6 | async-start | bytes 8650752 | tf_op jit(solution)/shard_map/reduce_scatter | solution.py:174
  207.6 64.1 %copy-start.10 = (bf16[255,512]{1,0:T(8,128)(2,1)S(1)}, bf16[255,512]{1,0:T(8,128)(2,1)}, u32[]{:S(2)}) copy-start(bf16[255,512]{1,0:T(8,128)(2,1)} %copy-done.9) | copy-start | bytes 783364
  207.6 1090.8 %all-reduce.9.cloned.1.call-start = ((), (), s32[]{:S(2)}) async-start(), calls=%async_computation.10 | async-start | bytes 1179648 | tf_op jit(solution)/shard_map/psum | solution.py:179
  (31 other events, 136.1 us)
Sparse Core Ops, SparseCore 0:
  168.1 219.9 reduce-scatter.12
  392.2 165.1 all-reduce.6
  561.2 211.0 reduce-scatter.6
  776.5 219.9 reduce-scatter.10
  1000.4 228.0 reduce-scatter.8
  1231.6 66.7 all-reduce.8
where the time goes:
time: 1310 us
  waiting for transfers between devices  995 us (76%)
  blocking collectives  133 us (10%)
  local copies, waits for them, and re-layouts  61.4 us (5%)
  other arithmetic  51.9 us (4%)
  matrix products  27.9 us (2%)
  starting transfers between devices  25.6 us (2%)
  between operations  16.8 us (1%)
    unnamed x8, waiting for transfers between devices  254 us
    reduce_scatter x1, waiting for transfers between devices, per_device(): lax.psum_scatter(in_term, 'tm', scatter_dimension=0, tiled=True)  232 us
    reduce_scatter x1, waiting for transfers between devices, per_device(): lax.psum_scatter(out_term, 'tm', scatter_dimension=0, tiled=True)  224 us
    reduce_scatter x1, waiting for transfers between devices, per_device(): lax.psum_scatter(proj_term, 'tm', scatter_dimension=0, tiled=True)  213 us
    psum x1, waiting for transfers between devices, per_device(): lax.psum((summed[0], summed[1], summed[2], summed[3], summed[4], summed[5...  68.8 us
    unnamed x1, blocking collectives  58.7 us
    all_gather x1, blocking collectives, per_device(): lax.all_gather(order, 'tm', axis=0, tiled=True).reshape(owners, frames)  47.6 us
    scatter x1, local copies, waits for them, and re-layouts, per_device(): slot_of_frame = jnp.zeros((frames,), jnp.int32).at[target.reshape(-1)].se...  30.6 us
  transfers between devices with their start and end apart: 12, of which 7 were waited for; matrix products, arithmetic and copies ran while one was open for 9% of the time, Pallas kernels for 0%

commit v1 on v0

v1 whole, which is shorter than its diff:
```python
import functools
import math

import jax
import jax.numpy as jnp
from jax import lax
from jax.experimental import pallas as pl
from jax.experimental.pallas import tpu as pltpu
from jax.sharding import PartitionSpec as P

EPS = 1e-05
MESH = pl.DeviceIdType.MESH
BF, F32 = jnp.bfloat16, jnp.float32

F = 256
D = 1024
CF = 512
KW = 31
HALF = 15
H = 16
EXT = F + 2 * H
PAD = EXT + 8
NEXT = F + 8
NEXT16 = F + 16
CAP = 16
NTM, NZ, NX, NY, NC = 32, 8, 4, 4, 2
IDX = 128
PART_ROWS = (32, 64, 48)

NT = (((1,), (1,)), ((), ()))


def dot(a, b):
    return jnp.dot(a, b, preferred_element_type=F32)


def dot_nt(a, b):
    return lax.dot_general(a, b, NT, preferred_element_type=F32)


def block(i, size):
    return pl.ds(pl.multiple_of(i * size, size), size)


def loop(n, body):
    def step(i, carry):
        body(i)
        return carry

    lax.fori_loop(0, n, step, 0)


class Place:
    def __init__(self):
        self.dp = lax.axis_index("dp")
        self.tm = lax.axis_index("tm")
        self.y = lax.div(self.dp, 2)
        self.c = lax.rem(self.dp, 2)
        self.z = lax.div(self.tm, NX)
        self.x = lax.rem(self.tm, NX)

    def at_c(self):
        return (self.y * 2 + (1 - self.c), self.tm)

    def at_y(self, d):
        return (lax.rem(self.y + d, NY) * 2 + self.c, self.tm)

    def at_x(self, d):
        return (self.dp, self.z * NX + lax.rem(self.x + d, NX))

    def at_z(self, d):
        return (self.dp, lax.rem(self.z + d, NZ) * NX + self.x)

    def at_dp(self, d):
        return (lax.rem(self.dp + d, 8), self.tm)

    def at_tm(self, d):
        return (self.dp, lax.rem(self.tm + d, NTM))


def remote(src, dst, send, recv, device):
    return pltpu.make_async_remote_copy(
        src_ref=src, dst_ref=dst, send_sem=send, recv_sem=recv, device_id=device, device_id_type=MESH
    )


def part_scratch(rows):
    tile = (rows, 128)
    return [
        pltpu.VMEM((NC, NY, NZ, NX) + tile, BF),
        pltpu.VMEM((NY, NZ, NX) + tile, BF),
        pltpu.VMEM((3, 4, NX) + tile, BF),
        pltpu.VMEM((3, NY, 4) + tile, BF),
        pltpu.VMEM((4, NX) + tile, BF),
        pltpu.VMEM((NY, 4) + tile, BF),
        pltpu.VMEM((3, 4) + tile, BF),
        pltpu.VMEM((3, 4) + tile, BF),
        pltpu.VMEM((NZ,) + tile, BF),
        pltpu.VMEM((7,) + tile, BF),
        pltpu.VMEM((8,) + tile, BF),
        pltpu.SemaphoreType.DMA((27,)),
        pltpu.SemaphoreType.DMA((27,)),
    ]


class Part:
    def __init__(self, at, refs):
        self.at = at
        (self.g, self.r0, self.r1p, self.r1q, self.a1p, self.a1q, self.r2p, self.r2q) = refs[:8]
        (self.a2, self.r3, self.fin, self.send, self.recv) = refs[8:]
        self.sent = []

    def copy(self, i, src, dst, device):
        return remote(src, dst, self.send.at[i], self.recv.at[i], device)

    def go(self, copies):
        for one in copies:
            one.start()
        self.sent += copies

    def s0(self):
        return [self.copy(0, self.g.at[1 - self.at.c], self.r0, self.at.at_c())]

    def s1(self):
        at, out = self.at, []
        for d in (1, 3, 2):
            y = lax.rem(at.y + d, NY)
            x = lax.rem(at.x + d, NX)
            out.append(
                self.copy(d, self.g.at[at.c, y, pl.ds(0, 4)], self.r1p.at[d - 1], at.at_y(d))
            )
            out.append(
                self.copy(
                    3 + d, self.g.at[at.c, :, pl.ds(4, 4), x], self.r1q.at[d - 1], at.at_x(d)
                )
            )
        return out

    def s2(self):
        at, out = self.at, []
        for d in (1, 3, 2):
            y = lax.rem(at.y + d, NY)
            x = lax.rem(at.x + d, NX)
            out.append(self.copy(6 + d, self.a1p.at[:, x], self.r2p.at[d - 1], at.at_x(d)))
            out.append(self.copy(9 + d, self.a1q.at[y], self.r2q.at[d - 1], at.at_y(d)))
        return out

    def s3(self):
        at, out = self.at, []
        for d in (1, 7, 2, 6, 3, 5, 4):
            z = lax.rem(at.z + d, NZ)
            out.append(self.copy(12 + d, self.a2.at[z], self.r3.at[d - 1], at.at_z(d)))
        return out

    def s4(self):
        at, out = self.at, []
        mine = at.c * NY + at.y
        for d in range(1, 8):
            out.append(self.copy(19 + d, self.fin.at[mine], self.fin.at[mine], at.at_dp(d)))
        return out

    def arrived(self, copies):
        for one in copies:
            one.wait_recv()

    def start(self):
        self.go(self.s0())

    def over_core(self):
        self.arrived(self.s0())
        c = self.at.c

        def add(i):
            y, z = lax.div(i, NZ), lax.rem(i, NZ)
            self.g[c, y, z] = (self.g[c, y, z].astype(F32) + self.r0[y, z].astype(F32)).astype(BF)

        loop(NY * NZ, add)
        self.go(self.s1())

    def over_first(self):
        self.arrived(self.s1())
        c, y, x = self.at.c, self.at.y, self.at.x

        def add(i):
            total = self.g[c, y, i].astype(F32)
            other = self.g[c, i, pl.ds(4, 4), x].astype(F32)
            for d in range(3):
                total = total + self.r1p[d, i].astype(F32)
                other = other + self.r1q[d, i].astype(F32)
            self.a1p[i] = total.astype(BF)
            self.a1q[i] = other.astype(BF)

        loop(4, add)
        self.go(self.s2())

    def over_second(self):
        self.arrived(self.s2())
        y, x = self.at.y, self.at.x

        def add(i):
            total = self.a1p[i, x].astype(F32)
            other = self.a1q[y, i].astype(F32)
            for d in range(3):
                total = total + self.r2p[d, i].astype(F32)
                other = other + self.r2q[d, i].astype(F32)
            self.a2[i] = total.astype(BF)
            self.a2[4 + i] = other.astype(BF)

        loop(4, add)
        self.go(self.s3())

    def over_z(self, factor):
        self.arrived(self.s3())
        total = self.a2[self.at.z].astype(F32)
        for d in range(7):
            total = total + self.r3[d].astype(F32)
        self.fin[self.at.c * NY + self.at.y] = (total * factor).astype(BF)
        self.go(self.s4())

    def gathered(self):
        self.arrived(self.s4())

    def close(self):
        for one in self.sent:
            one.wait_send()


def kernel(
    lengths, route, rows_grad, conv_pre, conv_in, conv_w, proj_w, in_w, depth_w, depth_gain, out_w,
    o_input, o_conv, o_proj, o_in, o_misc, o_out,
    outgoing, incoming, pre, cin_halo, linked, seg, act, slope, feat, linear, sigma, glu, mixed,
    swish_t, dfac, inv, dmix, up, hot, taps, gainsum, dj, df, dpre, feat_t, act_t, sel_t, pairs, dgs,
    a2a_send, a2a_recv, halo_send, halo_recv,
    *parts_refs,
):
    at = Place()
    tm = at.tm
    p_out, p_in, p_rest = (Part(at, parts_refs[13 * i : 13 * i + 13]) for i in range(3))
    left, right = (at.dp, lax.rem(tm + NTM - 1, NTM)), (at.dp, lax.rem(tm + 1, NTM))

    barrier = pltpu.get_barrier_semaphore()

    def greet(d):
        pl.semaphore_signal(barrier, inc=1, device_id=at.at_tm(d + 1), device_id_type=MESH)

    loop(NTM - 1, greet)
    for d in range(1, 8):
        pl.semaphore_signal(barrier, inc=1, device_id=at.at_dp(d), device_id_type=MESH)

    order = route[...]
    owner_row = lax.div(order, F).astype(F32)
    local_row = lax.rem(order, F).astype(F32) + 1.0
    sub = lax.broadcasted_iota(jnp.int32, (F, F), 0)
    lane = lax.broadcasted_iota(jnp.int32, (F, F), 1)
    owners = jnp.broadcast_to(owner_row, (F, F))
    owner_col = jnp.sum(jnp.where(sub == lane, owners, 0.0), axis=1, keepdims=True)
    local_col = jnp.sum(
        jnp.where(sub == lane, jnp.broadcast_to(local_row, (F, F)), 0.0), axis=1, keepdims=True
    )
    before = jnp.where((owners == owner_col) & (sub < lane), 1.0, 0.0)
    slot_row = owner_row * CAP + jnp.sum(before, axis=0, keepdims=True)
    slots = lax.broadcasted_iota(jnp.int32, (NTM * CAP, F), 0).astype(F32)
    hot[...] = jnp.where(slots == slot_row, 1.0, 0.0).astype(BF)

    def pack(j):
        outgoing[:, block(j, 256)] = dot(hot[...], rows_grad[:, block(j, 256)]).astype(BF)

    loop(4, pack)
    outgoing[:, D : D + IDX] = dot(
        hot[...], jnp.broadcast_to(local_col, (F, IDX)).astype(BF)
    ).astype(BF)

    pl.semaphore_wait(barrier, NTM - 1 + 7)

    halos = [
        remote(conv_pre.at[pl.ds(0, H)], pre.at[pl.ds(H + F, H)], halo_send.at[0], halo_recv.at[0], left),
        remote(conv_pre.at[pl.ds(F - H, H)], pre.at[pl.ds(0, H)], halo_send.at[1], halo_recv.at[1], right),
        remote(conv_in.at[pl.ds(2 * F - 16, 16)], cin_halo, halo_send.at[2], halo_recv.at[2], right),
    ]
    for one in halos:
        one.start()

    def routed(d):
        other = lax.rem(tm + d, NTM)
        return remote(
            outgoing.at[block(other, CAP)],
            incoming.at[block(tm, CAP)],
            a2a_send.at[d],
            a2a_recv.at[d],
            (at.dp, other),
        )

    loop(NTM - 1, lambda d: routed(d + 1).start())
    incoming[block(tm, CAP)] = outgoing[block(tm, CAP)]

    bound0 = lengths[0, 0]
    bound1 = bound0 + lengths[0, 1]
    bound2 = bound1 + lengths[0, 2]
    bound3 = bound2 + lengths[0, 3]
    pos = tm * F - H + lax.broadcasted_iota(jnp.int32, (PAD, 128), 0)
    number = sum((pos >= b).astype(jnp.int32) for b in (bound0, bound1, bound2, bound3))
    inside = (pos >= 0) & (pos < F * NTM)
    seg[...] = jnp.where(inside, number, -1)
    for k in range(KW):
        linked[k] = jnp.where(seg[pl.ds(H + k - HALF, NEXT)] == seg[pl.ds(H, NEXT)], 1.0, 0.0)
    taps[pl.ds(0, KW), :] = depth_w[...].astype(F32)
    glu[pl.ds(EXT, 8), :] = jnp.zeros((8, D), F32)
    dmix[pl.ds(EXT, 8), :] = jnp.zeros((8, D), F32)
    dj[pl.ds(F, 16), :] = jnp.zeros((16, 2 * D), BF)

    pre[pl.ds(H, F), :] = conv_pre[...]
    for one in halos[:2]:
        one.wait_recv()

    def gelu(i):
        rows = block(i, 32)
        v = pre[rows, :].astype(F32)
        half = 0.5 * (1.0 + lax.erf(v * (1.0 / math.sqrt(2.0))))
        act[rows, :] = (v * half).astype(BF)
        slope[rows, :] = half + v * jnp.exp(-0.5 * v * v) * (1.0 / math.sqrt(2.0 * math.pi))

    loop(EXT // 32, gelu)

    def features(j):
        feat[:, block(j, 256)] = dot(act[...], proj_w[:, block(j, 256)]).astype(BF)

    loop(4, features)

    def joined(j):
        lin = dot(feat[...], in_w[:, block(j, 256)])
        sig = jax.nn.sigmoid(dot(feat[...], in_w[:, block(4 + j, 256)]))
        linear[:, block(j, 256)] = lin
        sigma[:, block(j, 256)] = sig
        glu[pl.ds(0, EXT), block(j, 256)] = (lin * sig).astype(BF).astype(F32)

    loop(4, joined)

    def mix(j):
        cols = block(j, 128)
        for r in range(0, F, 64):
            total = jnp.zeros((64, 128), F32)
            for k in range(KW):
                total = total + taps[pl.ds(k, 1), cols] * (
                    glu[pl.ds(H + r + k - HALF, 64), cols] * linked[k, pl.ds(r, 64)]
                )
            mixed[pl.ds(r, 64), cols] = total

    loop(8, mix)
    gain = depth_gain[...].astype(F32)

    def norm_all(i):
        rows = block(i, 32)
        v = mixed[rows, :]
        v = v - jnp.mean(v, axis=1, keepdims=True)
        scale = 1.0 / jnp.sqrt(jnp.mean(v * v, axis=1, keepdims=True) + EPS)
        v = v * scale
        inv[rows, :] = jnp.broadcast_to(scale, (32, 128))
        mixed[rows, :] = v
        scaled = v * gain
        s = jax.nn.sigmoid(scaled)
        dfac[rows, :] = s * (1.0 + scaled * (1.0 - s))
        dmix[pl.ds(pl.multiple_of(H + i * 32, 16), 32), :] = scaled * s

    loop(8, norm_all)

    def turn(j):
        cols = block(j, 256)
        swish_t[cols, :] = jnp.transpose(dmix[pl.ds(H, F), cols]).astype(BF)
        feat_t[cols, :] = jnp.transpose(feat[pl.ds(H, F), cols].astype(F32)).astype(BF)

    loop(4, turn)

    def turn_act(j):
        cols = block(j, 256)
        act_t[cols, :] = jnp.transpose(act[pl.ds(H, F), cols].astype(F32)).astype(BF)

    loop(2, turn_act)

    loop(NTM - 1, lambda d: routed(d + 1).wait_recv())
    number = incoming[:, D : D + IDX].astype(F32)
    number = jnp.concatenate([number, number], axis=1)
    wanted = lax.broadcasted_iota(jnp.int32, (NTM * CAP, F), 1).astype(F32) + 1.0
    chosen = jnp.where(number == wanted, 1.0, 0.0)
    sel_t[...] = jnp.transpose(chosen).astype(BF)

    def place(j):
        up[pl.ds(0, F), block(j, 256)] = dot(sel_t[...], incoming[:, block(j, 256)]).astype(BF)

    loop(4, place)
    edge_up = remote(up.at[pl.ds(0, 16)], up.at[pl.ds(F, 16)], halo_send.at[3], halo_recv.at[3], left)
    edge_up.start()

    def dswish(j):
        cols = block(j, 256)
        dfac[:, cols] = dfac[:, cols] * dot_nt(up[pl.ds(0, F), :], out_w[block(j, 256), :])

    loop(4, dswish)
    gainsum[...] = jnp.zeros((8, D), F32)

    def dnorm(i):
        rows = block(i, 32)
        ds = dfac[rows, :]
        v = mixed[rows, :]
        dv = ds * v
        gainsum[...] += dv[0:8] + dv[8:16] + dv[16:24] + dv[24:32]
        q = ds * gain
        q = q - jnp.mean(q, axis=1, keepdims=True) - v * jnp.mean(q * v, axis=1, keepdims=True)
        dmix[pl.ds(pl.multiple_of(H + i * 32, 16), 32), :] = inv[rows, pl.ds(0, 1)] * q

    loop(8, dnorm)
    edges = [
        remote(dmix.at[pl.ds(H, H)], dmix.at[pl.ds(H + F, H)], halo_send.at[4], halo_recv.at[4], left),
        remote(dmix.at[pl.ds(F, H)], dmix.at[pl.ds(0, H)], halo_send.at[5], halo_recv.at[5], right),
    ]
    for one in edges:
        one.start()

    def out_terms(half):
        def body(i):
            b = half * 2 + i
            cols = block(b, 256)
            term = dot(swish_t[...], up[pl.ds(0, F), cols]).astype(BF)
            for s in range(2):
                y = i * 2 + s
                p_out.g[half, y] = term[:, 128 * s : 128 * s + 128].reshape(NZ, NX, 32, 128)

        loop(2, body)

    out_terms(1 - at.c)
    p_out.start()
    out_terms(at.c)

    def depth(j):
        cols = block(j, 128)
        for k in range(KW):
            total = jnp.zeros((8, 128), F32)
            for r in range(0, F, 64):
                term = (
                    glu[pl.ds(H + r + k - HALF, 64), cols]
                    * linked[k, pl.ds(r, 64)]
                    * dmix[pl.ds(H + r, 64), cols]
                )
                total = total + jnp.sum(term.reshape(8, 8, 128), axis=0)
            dgs[k // 8, pl.ds(k % 8, 1), cols] = jnp.sum(total, axis=0, keepdims=True)

    dgs[:, pl.ds(8, 8), :] = jnp.zeros((4, 8, D), F32)
    loop(8, depth)
    dgs[3, pl.ds(7, 1), :] = jnp.sum(gainsum[...], axis=0, keepdims=True)
    p_out.over_core()

    for one in edges:
        one.wait_recv()
    edge_up.wait_recv()

    def dconv(j):
        cols = block(j, 128)
        gates = block(8 + j, 128)
        for r, size in ((0, 64), (64, 64), (128, 64), (192, 64), (256, 8)):
            total = jnp.zeros((size, 128), F32)
            for k in range(KW):
                total = total + taps[pl.ds(KW - 1 - k, 1), cols] * (
                    dmix[pl.ds(H + r + k - HALF, size), cols] * linked[k, pl.ds(r, size)]
                )
            sig = sigma[pl.ds(H + r, size), cols]
            ds = total * sig
            dg = ds * linear[pl.ds(H + r, size), cols] * (1.0 - sig)
            if size == 8:
                zero = jnp.zeros((8, 128), F32)
                ds = jnp.concatenate([ds, zero], axis=0)
                dg = jnp.concatenate([dg, zero], axis=0)
            dj[pl.ds(r, max(size, 16)), cols] = ds.astype(BF)
            dj[pl.ds(r, max(size, 16)), gates] = dg.astype(BF)

    loop(8, dconv)
    p_out.over_first()

    def in_terms(half):
        def body(y):
            term = dot(feat_t[...], dj[pl.ds(0, F), block(half * 4 + y, 256)]).astype(BF)
            for s in range(2):
                p_in.g[half, y, :, :, pl.ds(32 * s, 32), :] = term[
                    :, 128 * s : 128 * s + 128
                ].reshape(NZ, NX, 32, 128)

        loop(4, body)

    in_terms(1 - at.c)
    p_in.start()
    in_terms(at.c)

    def dfeatures(j):
        cols = block(j, 256)
        df[:, cols] = (up[:, cols].astype(F32) + dot_nt(dj[...], in_w[cols, :])).astype(BF)

    loop(4, dfeatures)
    p_in.over_core()

    def dpres(j):
        cols = block(j, 256)
        dpre[:, cols] = (dot_nt(df[...], proj_w[cols, :]) * slope[pl.ds(H, NEXT16), cols]).astype(BF)

    loop(2, dpres)

    halos[2].wait_recv()
    r_f = lax.broadcasted_iota(jnp.int32, (F, 2 * F), 0)
    c_f = lax.broadcasted_iota(jnp.int32, (F, 2 * F), 1)
    r_h = lax.broadcasted_iota(jnp.int32, (F, 16), 0)
    c_h = lax.broadcasted_iota(jnp.int32, (F, 16), 1)
    first = (r_h == 0) & (c_h == 15) & (tm > 0)

    def one_hot(mask):
        return jnp.where(mask, 1.0, 0.0).astype(BF)

    def rest_terms(half):
        def body(i):
            cols = block(half * 2 + i, 256)
            term = dot(act_t[...], df[pl.ds(0, F), cols]).astype(BF)
            for s in range(2):
                y = i * 2 + s
                p_rest.g[half, y, :, :, pl.ds(0, 16), :] = term[
                    :, 128 * s : 128 * s + 128
                ].reshape(NZ, NX, 16, 128)

        loop(2, body)

    def conv_terms(core, row):
        def body(i):
            term = dot(pairs[...], dpre[pl.ds(0, F), block(i, 256)]).astype(BF)
            for s in range(2):
                p_rest.g[core, i * 2 + s, :, :, pl.ds(row, 16), :] = term[
                    :, 128 * s : 128 * s + 128
                ].reshape(NZ, NX, 16, 128)

        loop(2, body)

    rest_terms(0)
    rest_terms(1)
    for tap, core, row in ((0, 0, 16), (1, 0, 32), (2, 1, 16)):
        rows = dot(one_hot(c_f == 2 * r_f + tap - 1), conv_in[...])
        if tap == 0:
            rows = rows + dot(one_hot(first), cin_halo[...])
        pairs[...] = jnp.transpose(rows).astype(BF)
        conv_terms(core, row)
    for z in range(NZ):
        small = dgs[:, :, 128 * z : 128 * z + 128].astype(BF)
        for x in range(NX):
            p_rest.g[1, :, z, x, pl.ds(32, 16), :] = small
    p_rest.start()
    p_out.over_second()
    p_in.over_first()

    r_o = lax.broadcasted_iota(jnp.int32, (2 * F, NEXT16), 0)
    c_o = lax.broadcasted_iota(jnp.int32, (2 * F, NEXT16), 1)
    here = dot(one_hot(r_o == 2 * c_o), dpre[...]).astype(BF)
    here_odd = dot(one_hot(r_o == 2 * c_o + 1), dpre[...]).astype(BF)
    ahead = (r_o == 2 * c_o - 1) & ((c_o < F) | (tm < NTM - 1))
    ahead = dot(one_hot(ahead), dpre[...]).astype(BF)
    o_input[...] = dot_nt(here, conv_w[1])
    o_input[...] += dot_nt(here_odd, conv_w[2])
    o_input[...] += dot_nt(ahead, conv_w[0])

    factor = 1.0 / math.sqrt(F * NTM * 8)
    p_rest.over_core()
    p_out.over_z(factor)
    p_in.over_second()
    p_rest.over_first()
    p_in.over_z(factor)
    p_rest.over_second()
    p_out.gathered()
    for b in range(8):
        o_out[:, 128 * b : 128 * b + 128] = p_out.fin[b].astype(F32)
    p_rest.over_z(factor)
    p_in.gathered()
    for b in range(8):
        for s in range(2):
            o_in[:, 256 * b + 128 * s : 256 * b + 128 * s + 128] = p_in.fin[
                b, pl.ds(32 * s, 32)
            ].astype(F32)
    p_rest.gathered()
    for b in range(8):
        o_proj[:, 128 * b : 128 * b + 128] = p_rest.fin[b, pl.ds(0, 16)].astype(F32)
    for y in range(NY):
        cols = pl.ds(128 * y, 128)
        o_conv[0, :, cols] = p_rest.fin[y, pl.ds(16, 16)].astype(F32)
        o_conv[1, :, cols] = p_rest.fin[y, pl.ds(32, 16)].astype(F32)
        o_conv[2, :, cols] = p_rest.fin[NY + y, pl.ds(16, 16)].astype(F32)
        small = p_rest.fin[NY + y, pl.ds(32, 16)].astype(F32)[0:8]
        mine = jnp.zeros((8, 32), F32)
        for x in range(NX):
            mine = mine + jnp.where(at.x == x, small[:, 32 * x : 32 * x + 32], 0.0)
        o_misc[pl.ds(8 * y, 8), :] = mine

    loop(NTM - 1, lambda d: routed(d + 1).wait_send())
    for one in halos + [edge_up] + edges:
        one.wait_send()
    for part in (p_out, p_in, p_rest):
        part.close()


def per_device(
    grad_attn, route, lengths, conv_pre, conv_in, conv_w, proj_w, in_w, depth_w, depth_gain, out_w
):
    vmem = pl.BlockSpec(memory_space=pltpu.VMEM)
    smem = pl.BlockSpec(memory_space=pltpu.SMEM)
    scratch = [
        pltpu.VMEM((NTM * CAP, D + IDX), BF),
        pltpu.VMEM((NTM * CAP, D + IDX), BF),
        pltpu.VMEM((EXT, CF), BF),
        pltpu.VMEM((16, CF), BF),
        pltpu.VMEM((KW, NEXT, 128), F32),
        pltpu.VMEM((PAD, 128), jnp.int32),
        pltpu.VMEM((EXT, CF), BF),
        pltpu.VMEM((EXT, CF), F32),
        pltpu.VMEM((EXT, D), BF),
        pltpu.VMEM((EXT, D), F32),
        pltpu.VMEM((EXT, D), F32),
        pltpu.VMEM((PAD, D), F32),
        pltpu.VMEM((F, D), F32),
        pltpu.VMEM((D, F), BF),
        pltpu.VMEM((F, D), F32),
        pltpu.VMEM((F, 128), F32),
        pltpu.VMEM((PAD, D), F32),
        pltpu.VMEM((NEXT16, D), BF),
        pltpu.VMEM((NTM * CAP, F), BF),
        pltpu.VMEM((32, D), F32),
        pltpu.VMEM((8, D), F32),
        pltpu.VMEM((NEXT16, 2 * D), BF),
        pltpu.VMEM((NEXT16, D), BF),
        pltpu.VMEM((NEXT16, CF), BF),
        pltpu.VMEM((D, F), BF),
        pltpu.VMEM((CF, F), BF),
        pltpu.VMEM((F, NTM * CAP), BF),
        pltpu.VMEM((CF, F), BF),
        pltpu.VMEM((4, 16, D), F32),
        pltpu.SemaphoreType.DMA((NTM,)),
        pltpu.SemaphoreType.DMA((NTM,)),
        pltpu.SemaphoreType.DMA((6,)),
        pltpu.SemaphoreType.DMA((6,)),
    ]
    for rows in PART_ROWS:
        scratch += part_scratch(rows)
    outs = pl.pallas_call(
        kernel,
        out_shape=[
            jax.ShapeDtypeStruct((2 * F, CF), F32),
            jax.ShapeDtypeStruct((3, 16, CF), F32),
            jax.ShapeDtypeStruct((16, D), F32),
            jax.ShapeDtypeStruct((32, 2 * D), F32),
            jax.ShapeDtypeStruct((32, 32), F32),
            jax.ShapeDtypeStruct((32, D), F32),
        ],
        in_specs=[smem] + [vmem] * 10,
        out_specs=[vmem] * 6,
        scratch_shapes=scratch,
        compiler_params=pltpu.CompilerParams(
            collective_id=0, has_side_effects=True, vmem_limit_bytes=62 * 2**20
        ),
    )(
        lengths, route, grad_attn[0], conv_pre[0], conv_in[0], conv_w, proj_w, in_w, depth_w,
        depth_gain[None], out_w,
    )
    o_input, o_conv, o_proj, o_in, o_misc, o_out = outs
    return (o_input[None], o_conv, o_proj, o_in, o_misc[:KW], o_misc[KW], o_out)


def solution(mesh):
    placed = (
        P("dp", "tm", None),
        P("dp", "tm"),
        P("dp", None),
        P("dp", "tm", None),
        P("dp", "tm", None),
        P(),
        P(),
        P(),
        P(),
        P(),
        P(),
    )
    return jax.shard_map(
        per_device,
        mesh=mesh,
        in_specs=placed,
        out_specs=(
            P("dp", "tm", None),
            P(None, "tm", None),
            P("tm", None),
            P("tm", None),
            P(None, "tm"),
            P("tm"),
            P("tm", None),
        ),
        check_vma=False,
    )
```

time: 1310 us -> 132 us (0.10)
  waiting for transfers between devices: 995 us -> 0 us
  blocking collectives: 133 us -> 0 us
  Pallas kernels: 0 us -> 124 us
  local copies, waits for them, and re-layouts: 61.4 us -> 8.03 us
  other arithmetic: 51.9 us -> 0 us
  matrix products: 27.9 us -> 0 us
  starting transfers between devices: 25.6 us -> 0 us
  between operations: 16.8 us -> 0.69 us
    reduce_scatter x3 -> x0, waiting for transfers between devices: 670 us -> none  [the longest x1 232 us: per_device(): lax.psum_scatter(in_term, 'tm', scatter_dimension=0, tiled=True)]
    unnamed x8 -> x0, waiting for transfers between devices: 254 us -> none
    pallas_call x0 -> x1, Pallas kernels: none -> 124 us  [per_device(): pl.pallas_call(kernel, out_shape=[jax.ShapeDtypeStruct((2 * F, CF), F32),...]
    psum x1 -> x0, waiting for transfers between devices: 68.8 us -> none  [per_device(): lax.psum((summed[0], summed[1], summed[2], summed[3], summed[4], summed[5...]
    unnamed x1 -> x0, blocking collectives: 58.7 us -> none
    all_gather x1 -> x0, blocking collectives: 47.6 us -> none  [per_device(): lax.all_gather(order, 'tm', axis=0, tiled=True).reshape(owners, frames)]
    scatter x2 -> x0, local copies, waits for them, and re-layouts: 33.3 us -> none  [the longest x1 30.6 us: per_device(): slot_of_frame = jnp.zeros((frames,), jnp.int32).at[target.reshape(-1)].se...]
    reduce_sum x11 -> x0, other arithmetic: 28.4 us -> none  [the longest x6 17.7 us: per_device(): jnp.sum(glu_wide[offset:offset + frames].astype(jnp.float32) * dmixed_f *...]
  transfers between devices with their start and end apart: 12 -> 0, of which waited for: 7 -> 0; matrix products, arithmetic and copies ran while one was open for 9% -> 0% of each run, Pallas kernels for 0% -> 0%
where the time goes in v1:
time: 132 us
  Pallas kernels  124 us (94%)
  local copies, waits for them, and re-layouts  8.03 us (6%)
    pallas_call x1, Pallas kernels, per_device(): pl.pallas_call(kernel, out_shape=[jax.ShapeDtypeStruct((2 * F, CF), F32),...  124 us
    unnamed x16, local copies, waits for them, and re-layouts  5.52 us

profile of v1, /device:TPU:1, one launch (start us, length us, event | category | flops | bytes accessed | tf_op | source)
XLA Modules:
  0.0 132.3 jit_solution(15924011733103420572)
XLA Ops:
  0.6 1.3 broadcast_in_dim.6.depth_gain
  1.9 123.6 %shard_map.162 = (f32[512,512]{1,0:T(8,128)}, f32[3,16,512]{2,1,0:T(8,128)}, f32[16,1024]{1,0:T(8,128)}, f32[32,2048]{1,0:T(8,128)}, f32[32,32]{1,0:T(8,128)}, /*index=5*/f32[32,1024]{1,0:T(8,128)}) custom-call(s32[1,4]{1,0:T(1,128)} %lengths.1, s32[1,256]{1,0:T(1,128)} %route.1, bf16[256,1024]{1,0:T(8,128)(2,1)} %bitcast.8, bf16[256,512]{1,0:T(8,128)(2,1)} %bitcast.10, ...), custom_call_target="tpu_custom_call" | custom-call | tf_op jit(solution)/shard_map/pallas_call | solution.py:642
  125.5 0.0 copy-start.2
  125.5 0.0 copy-start.3
  125.5 0.0 copy-start
  125.5 0.0 copy-start.4
  125.5 0.0 copy-start.1
  125.5 1.2 slice_bitcast_fusion
  126.8 2.3 %copy.24 = f32[1,512,512]{2,1,0:T(8,128)} copy(f32[1,512,512]{2,1,0:T(8,128)} %bitcast.7) | data formatting | bytes 2097152
  129.0 0.0 copy-done.2
  129.0 0.6 copy.25
  129.7 0.0 copy-done.3
  129.7 0.6 copy.26
  130.3 0.0 copy-done
  130.3 0.7 copy.27
  131.0 0.0 copy-done.4
  131.0 0.6 copy.28
  131.6 0.0 copy-done.1
  131.6 0.7 copy.29
Async XLA Ops:
  125.5 3.6 %copy-start.2 = (f32[3,16,512]{2,1,0:T(8,128)S(1)}, f32[3,16,512]{2,1,0:T(8,128)}, u32[]{:S(2)}) copy-start(f32[3,16,512]{2,1,0:T(8,128)} %get-tuple-element.27) | copy-start | bytes 294916
  125.5 4.2 %copy-start.3 = (f32[16,1024]{1,0:T(8,128)S(1)}, f32[16,1024]{1,0:T(8,128)}, u32[]{:S(2)}) copy-start(f32[16,1024]{1,0:T(8,128)} %get-tuple-element.28) | copy-start | bytes 196612
  125.5 4.8 %copy-start = (f32[32,2048]{1,0:T(8,128)S(1)}, f32[32,2048]{1,0:T(8,128)}, u32[]{:S(2)}) copy-start(f32[32,2048]{1,0:T(8,128)} %get-tuple-element.29) | copy-start | bytes 786436
  125.5 5.5 %copy-start.4 = (f32[32,32]{1,0:T(8,128)S(1)}, f32[32,32]{1,0:T(8,128)}, u32[]{:S(2)}) copy-start(f32[32,32]{1,0:T(8,128)} %get-tuple-element.17) | copy-start | bytes 12292
  125.5 6.1 %copy-start.1 = (f32[32,1024]{1,0:T(8,128)S(1)}, f32[32,1024]{1,0:T(8,128)}, u32[]{:S(2)}) copy-start(f32[32,1024]{1,0:T(8,128)} %get-tuple-element.32) | copy-start | bytes 393220

commit v2 on v1

--- a/solution.py
+++ b/solution.py
@@ -50,6 +50,15 @@
     lax.fori_loop(0, n, step, 0)
 
 
+def shift_all(shifts, ref, cols):
+    for shift in range(8):
+        shifts[shift] = ref[pl.ds(H - HALF + shift, EXT), cols]
+
+
+def shifted(shifts, tap, start, size):
+    return shifts[tap % 8, pl.ds(start + tap - tap % 8, size)]
+
+
 class Place:
     def __init__(self):
         self.dp = lax.axis_index("dp")
@@ -89,8 +98,8 @@
     return [
         pltpu.VMEM((NC, NY, NZ, NX) + tile, BF),
         pltpu.VMEM((NY, NZ, NX) + tile, BF),
-        pltpu.VMEM((3, 4, NX) + tile, BF),
-        pltpu.VMEM((3, NY, 4) + tile, BF),
+        pltpu.VMEM((3, 2, 2, NX) + tile, BF),
+        pltpu.VMEM((3, 2, NY, 2) + tile, BF),
         pltpu.VMEM((4, NX) + tile, BF),
         pltpu.VMEM((NY, 4) + tile, BF),
         pltpu.VMEM((3, 4) + tile, BF),
@@ -98,8 +107,8 @@
         pltpu.VMEM((NZ,) + tile, BF),
         pltpu.VMEM((7,) + tile, BF),
         pltpu.VMEM((8,) + tile, BF),
-        pltpu.SemaphoreType.DMA((27,)),
-        pltpu.SemaphoreType.DMA((27,)),
+        pltpu.SemaphoreType.DMA((33,)),
+        pltpu.SemaphoreType.DMA((33,)),
     ]
 
 
@@ -121,42 +130,60 @@
     def s0(self):
         return [self.copy(0, self.g.at[1 - self.at.c], self.r0, self.at.at_c())]
 
-    def s1(self):
-        at, out = self.at, []
-        for d in (1, 3, 2):
-            y = lax.rem(at.y + d, NY)
-            x = lax.rem(at.x + d, NX)
-            out.append(
-                self.copy(d, self.g.at[at.c, y, pl.ds(0, 4)], self.r1p.at[d - 1], at.at_y(d))
-            )
-            out.append(
-                self.copy(
-                    3 + d, self.g.at[at.c, :, pl.ds(4, 4), x], self.r1q.at[d - 1], at.at_x(d)
-                )
-            )
-        return out
+    def rows_y(self, d, h):
+        return self.g.at[self.at.c, lax.rem(self.at.y + d, NY), pl.ds(2 * h, 2)]
+
+    def rows_x(self, d, h):
+        return self.g.at[self.at.c, :, pl.ds(4 + 2 * h, 2), lax.rem(self.at.x + d, NX)]
+
+    def s1_pass(self):
+        at = self.at
+        return [
+            self.copy(1, self.rows_y(2, 0), self.r1p.at[0, 0], at.at_y(1)),
+            self.copy(2, self.rows_y(2, 1), self.r1p.at[0, 1], at.at_y(3)),
+            self.copy(3, self.rows_x(2, 0), self.r1q.at[0, 0], at.at_x(1)),
+            self.copy(4, self.rows_x(2, 1), self.r1q.at[0, 1], at.at_x(3)),
+        ]
+
+    def s1_direct(self):
+        at = self.at
+        return [
+            self.copy(5, self.rows_y(1, 1), self.r1p.at[1, 1], at.at_y(1)),
+            self.copy(6, self.rows_y(3, 0), self.r1p.at[1, 0], at.at_y(3)),
+            self.copy(7, self.rows_x(1, 1), self.r1q.at[1, 1], at.at_x(1)),
+            self.copy(8, self.rows_x(3, 0), self.r1q.at[1, 0], at.at_x(3)),
+        ]
+
+    def s1_on(self):
+        at = self.at
+        return [
+            self.copy(9, self.rows_y(1, 0), self.r1p.at[2, 0], at.at_y(1)),
+            self.copy(10, self.rows_y(3, 1), self.r1p.at[2, 1], at.at_y(3)),
+            self.copy(11, self.rows_x(1, 0), self.r1q.at[2, 0], at.at_x(1)),
+            self.copy(12, self.rows_x(3, 1), self.r1q.at[2, 1], at.at_x(3)),
+        ]
 
     def s2(self):
         at, out = self.at, []
         for d in (1, 3, 2):
             y = lax.rem(at.y + d, NY)
             x = lax.rem(at.x + d, NX)
-            out.append(self.copy(6 + d, self.a1p.at[:, x], self.r2p.at[d - 1], at.at_x(d)))
-            out.append(self.copy(9 + d, self.a1q.at[y], self.r2q.at[d - 1], at.at_y(d)))
+            out.append(self.copy(12 + d, self.a1p.at[:, x], self.r2p.at[d - 1], at.at_x(d)))
+            out.append(self.copy(15 + d, self.a1q.at[y], self.r2q.at[d - 1], at.at_y(d)))
         return out
 
     def s3(self):
         at, out = self.at, []
         for d in (1, 7, 2, 6, 3, 5, 4):
             z = lax.rem(at.z + d, NZ)
-            out.append(self.copy(12 + d, self.a2.at[z], self.r3.at[d - 1], at.at_z(d)))
+            out.append(self.copy(18 + d, self.a2.at[z], self.r3.at[d - 1], at.at_z(d)))
         return out
 
     def s4(self):
         at, out = self.at, []
         mine = at.c * NY + at.y
         for d in range(1, 8):
-            out.append(self.copy(19 + d, self.fin.at[mine], self.fin.at[mine], at.at_dp(d)))
+            out.append(self.copy(25 + d, self.fin.at[mine], self.fin.at[mine], at.at_dp(d)))
         return out
 
     def arrived(self, copies):
@@ -170,27 +197,28 @@
         self.arrived(self.s0())
         c = self.at.c
 
-        def add(i):
-            y, z = lax.div(i, NZ), lax.rem(i, NZ)
-            self.g[c, y, z] = (self.g[c, y, z].astype(F32) + self.r0[y, z].astype(F32)).astype(BF)
-
-        loop(NY * NZ, add)
-        self.go(self.s1())
+        def add(y):
+            self.g[c, y] = (self.g[c, y].astype(F32) + self.r0[y].astype(F32)).astype(BF)
+
+        loop(NY, add)
+        self.go(self.s1_pass() + self.s1_direct())
+
+    def pass_on(self):
+        self.arrived(self.s1_pass())
+        for h, d in ((0, 1), (1, 3)):
+            rows = self.rows_y(d, h)
+            rows[...] = (rows[...].astype(F32) + self.r1p[0, h].astype(F32)).astype(BF)
+            rows = self.rows_x(d, h)
+            rows[...] = (rows[...].astype(F32) + self.r1q[0, h].astype(F32)).astype(BF)
+        self.go(self.s1_on())
 
     def over_first(self):
-        self.arrived(self.s1())
-        c, y, x = self.at.c, self.at.y, self.at.x
-
-        def add(i):
-            total = self.g[c, y, i].astype(F32)
-            other = self.g[c, i, pl.ds(4, 4), x].astype(F32)
-            for d in range(3):
-                total = total + self.r1p[d, i].astype(F32)
-                other = other + self.r1q[d, i].astype(F32)
-            self.a1p[i] = total.astype(BF)
-            self.a1q[i] = other.astype(BF)
-
-        loop(4, add)
+        self.arrived(self.s1_direct() + self.s1_on())
+        for h in range(2):
+            total = self.rows_y(0, h)[...].astype(F32) + self.r1p[1, h].astype(F32)
+            self.a1p[pl.ds(2 * h, 2)] = (total + self.r1p[2, h].astype(F32)).astype(BF)
+            total = self.rows_x(0, h)[...].astype(F32) + self.r1q[1, h].astype(F32)
+            self.a1q[:, pl.ds(2 * h, 2)] = (total + self.r1q[2, h].astype(F32)).astype(BF)
         self.go(self.s2())
 
     def over_second(self):
@@ -226,10 +254,12 @@
 
 
 def kernel(
-    lengths, route, rows_grad, conv_pre, conv_in, conv_w, proj_w, in_w, depth_w, depth_gain, out_w,
-    o_input, o_conv, o_proj, o_in, o_misc, o_out,
+    lengths, route, rows_grad, h_conv_pre, h_conv_in, h_conv_w, h_proj_w, h_in_w, depth_w, depth_gain,
+    h_out_w,
+    o_input, o_fin_out, o_fin_in, o_fin_rest,
     outgoing, incoming, pre, cin_halo, linked, seg, act, slope, feat, linear, sigma, glu, mixed,
-    swish_t, dfac, inv, dmix, up, hot, taps, gainsum, dj, df, dpre, feat_t, act_t, sel_t, pairs, dgs,
+    swish_t, dfac, inv, dmix, up, hot, taps, gainsum, dj, df, dpre, feat_t, act_t, sel_t, pairs, dgs, shifts,
+    conv_in, conv_w, proj_w, in_w, out_w, load_sem,
     a2a_send, a2a_recv, halo_send, halo_recv,
     *parts_refs,
 ):
@@ -237,6 +267,22 @@
     tm = at.tm
     p_out, p_in, p_rest = (Part(at, parts_refs[13 * i : 13 * i + 13]) for i in range(3))
     left, right = (at.dp, lax.rem(tm + NTM - 1, NTM)), (at.dp, lax.rem(tm + 1, NTM))
+
+    loads = [
+        pltpu.make_async_copy(src, dst, load_sem.at[i])
+        for i, (src, dst) in enumerate(
+            (
+                (h_conv_pre, pre.at[pl.ds(H, F)]),
+                (h_conv_in, conv_in),
+                (h_proj_w, proj_w),
+                (h_in_w, in_w),
+                (h_out_w, out_w),
+                (h_conv_w, conv_w),
+            )
+        )
+    ]
+    for one in loads:
+        one.start()
 
     barrier = pltpu.get_barrier_semaphore()
 
@@ -272,9 +318,11 @@
 
     pl.semaphore_wait(barrier, NTM - 1 + 7)
 
+    for one in loads[:2]:
+        one.wait()
     halos = [
-        remote(conv_pre.at[pl.ds(0, H)], pre.at[pl.ds(H + F, H)], halo_send.at[0], halo_recv.at[0], left),
-        remote(conv_pre.at[pl.ds(F - H, H)], pre.at[pl.ds(0, H)], halo_send.at[1], halo_recv.at[1], right),
+        remote(pre.at[pl.ds(H, H)], pre.at[pl.ds(H + F, H)], halo_send.at[0], halo_recv.at[0], left),
+        remote(pre.at[pl.ds(F, H)], pre.at[pl.ds(0, H)], halo_send.at[1], halo_recv.at[1], right),
         remote(conv_in.at[pl.ds(2 * F - 16, 16)], cin_halo, halo_send.at[2], halo_recv.at[2], right),
     ]
     for one in halos:
@@ -308,7 +356,8 @@
     dmix[pl.ds(EXT, 8), :] = jnp.zeros((8, D), F32)
     dj[pl.ds(F, 16), :] = jnp.zeros((16, 2 * D), BF)
 
-    pre[pl.ds(H, F), :] = conv_pre[...]
+    for one in loads[2:4]:
+        one.wait()
     for one in halos[:2]:
         one.wait_recv()
 
@@ -337,16 +386,16 @@
 
     def mix(j):
         cols = block(j, 128)
+        shift_all(shifts, glu, cols)
         for r in range(0, F, 64):
             total = jnp.zeros((64, 128), F32)
             for k in range(KW):
-                total = total + taps[pl.ds(k, 1), cols] * (
-                    glu[pl.ds(H + r + k - HALF, 64), cols] * linked[k, pl.ds(r, 64)]
-                )
+                rows = shifted(shifts, k, r, 64)
+                total = total + taps[pl.ds(k, 1), cols] * (rows * linked[k, pl.ds(r, 64)])
             mixed[pl.ds(r, 64), cols] = total
 
     loop(8, mix)
-    gain = depth_gain[...].astype(F32)
+    gain = depth_gain[...].astype(F32).reshape(1, D)
 
     def norm_all(i):
         rows = block(i, 32)
@@ -376,6 +425,22 @@
 
     loop(2, turn_act)
 
+    halos[2].wait_recv()
+    r_f = lax.broadcasted_iota(jnp.int32, (F, 2 * F), 0)
+    c_f = lax.broadcasted_iota(jnp.int32, (F, 2 * F), 1)
+    r_h = lax.broadcasted_iota(jnp.int32, (F, 16), 0)
+    c_h = lax.broadcasted_iota(jnp.int32, (F, 16), 1)
+    first = (r_h == 0) & (c_h == 15) & (tm > 0)
+
+    def one_hot(mask):
+        return jnp.where(mask, 1.0, 0.0).astype(BF)
+
+    for tap in range(3):
+        rows = dot(one_hot(c_f == 2 * r_f + tap - 1), conv_in[...])
+        if tap == 0:
+            rows = rows + dot(one_hot(first), cin_halo[...])
+        pairs[tap] = jnp.transpose(rows).astype(BF)
+
     loop(NTM - 1, lambda d: routed(d + 1).wait_recv())
     number = incoming[:, D : D + IDX].astype(F32)
     number = jnp.concatenate([number, number], axis=1)
@@ -389,6 +454,9 @@
     loop(4, place)
     edge_up = remote(up.at[pl.ds(0, 16)], up.at[pl.ds(F, 16)], halo_send.at[3], halo_recv.at[3], left)
     edge_up.start()
+
+    for one in loads[4:]:
+        one.wait()
 
     def dswish(j):
         cols = block(j, 256)
@@ -429,23 +497,6 @@
     out_terms(1 - at.c)
     p_out.start()
     out_terms(at.c)
-
-    def depth(j):
-        cols = block(j, 128)
-        for k in range(KW):
-            total = jnp.zeros((8, 128), F32)
-            for r in range(0, F, 64):
-                term = (
-                    glu[pl.ds(H + r + k - HALF, 64), cols]
-                    * linked[k, pl.ds(r, 64)]
-                    * dmix[pl.ds(H + r, 64), cols]
-                )
-                total = total + jnp.sum(term.reshape(8, 8, 128), axis=0)
-            dgs[k // 8, pl.ds(k % 8, 1), cols] = jnp.sum(total, axis=0, keepdims=True)
-
-    dgs[:, pl.ds(8, 8), :] = jnp.zeros((4, 8, D), F32)
-    loop(8, depth)
-    dgs[3, pl.ds(7, 1), :] = jnp.sum(gainsum[...], axis=0, keepdims=True)
     p_out.over_core()
 
     for one in edges:
@@ -455,11 +506,13 @@
     def dconv(j):
         cols = block(j, 128)
         gates = block(8 + j, 128)
+        shift_all(shifts, dmix, cols)
         for r, size in ((0, 64), (64, 64), (128, 64), (192, 64), (256, 8)):
             total = jnp.zeros((size, 128), F32)
             for k in range(KW):
+                rows = shifted(shifts, k, r, size)
                 total = total + taps[pl.ds(KW - 1 - k, 1), cols] * (
-                    dmix[pl.ds(H + r + k - HALF, size), cols] * linked[k, pl.ds(r, size)]
+                    rows * linked[k, pl.ds(r, size)]
                 )
             sig = sigma[pl.ds(H + r, size), cols]
             ds = total * sig
@@ -471,8 +524,9 @@
             dj[pl.ds(r, max(size, 16)), cols] = ds.astype(BF)
             dj[pl.ds(r, max(size, 16)), gates] = dg.astype(BF)
 
-    loop(8, dconv)
-    p_out.over_first()
+    loop(4, dconv)
+    p_out.pass_on()
+    loop(4, lambda j: dconv(4 + j))
 
     def in_terms(half):
         def body(y):
@@ -487,6 +541,7 @@
     in_terms(1 - at.c)
     p_in.start()
     in_terms(at.c)
+    p_out.over_first()
 
     def dfeatures(j):
         cols = block(j, 256)
@@ -500,16 +555,6 @@
         dpre[:, cols] = (dot_nt(df[...], proj_w[cols, :]) * slope[pl.ds(H, NEXT16), cols]).astype(BF)
 
     loop(2, dpres)
-
-    halos[2].wait_recv()
-    r_f = lax.broadcasted_iota(jnp.int32, (F, 2 * F), 0)
-    c_f = lax.broadcasted_iota(jnp.int32, (F, 2 * F), 1)
-    r_h = lax.broadcasted_iota(jnp.int32, (F, 16), 0)
-    c_h = lax.broadcasted_iota(jnp.int32, (F, 16), 1)
-    first = (r_h == 0) & (c_h == 15) & (tm > 0)
-
-    def one_hot(mask):
-        return jnp.where(mask, 1.0, 0.0).astype(BF)
 
     def rest_terms(half):
         def body(i):
@@ -523,9 +568,9 @@
 
         loop(2, body)
 
-    def conv_terms(core, row):
+    def conv_terms(tap, core, row):
         def body(i):
-            term = dot(pairs[...], dpre[pl.ds(0, F), block(i, 256)]).astype(BF)
+            term = dot(pairs[tap], dpre[pl.ds(0, F), block(i, 256)]).astype(BF)
             for s in range(2):
                 p_rest.g[core, i * 2 + s, :, :, pl.ds(row, 16), :] = term[
                     :, 128 * s : 128 * s + 128
@@ -535,19 +580,36 @@
 
     rest_terms(0)
     rest_terms(1)
+    p_in.pass_on()
     for tap, core, row in ((0, 0, 16), (1, 0, 32), (2, 1, 16)):
-        rows = dot(one_hot(c_f == 2 * r_f + tap - 1), conv_in[...])
-        if tap == 0:
-            rows = rows + dot(one_hot(first), cin_halo[...])
-        pairs[...] = jnp.transpose(rows).astype(BF)
-        conv_terms(core, row)
+        conv_terms(tap, core, row)
+    p_out.over_second()
+
+    def depth(j):
+        cols = block(j, 128)
+        shift_all(shifts, glu, cols)
+        total = [None] * KW
+        for r in range(0, F, 64):
+            grad = dmix[pl.ds(H + r, 64), cols]
+            for k in range(KW):
+                rows = shifted(shifts, k, r, 64)
+                term = jnp.sum((rows * linked[k, pl.ds(r, 64)] * grad).reshape(8, 8, 128), axis=0)
+                total[k] = term if r == 0 else total[k] + term
+        for k in range(KW):
+            dgs[k // 8, pl.ds(k % 8, 1), cols] = jnp.sum(total[k], axis=0, keepdims=True)
+
+    dgs[:, pl.ds(8, 8), :] = jnp.zeros((4, 8, D), F32)
+    loop(8, depth)
+    dgs[3, pl.ds(7, 1), :] = jnp.sum(gainsum[...], axis=0, keepdims=True)
+    p_in.over_first()
     for z in range(NZ):
         small = dgs[:, :, 128 * z : 128 * z + 128].astype(BF)
         for x in range(NX):
             p_rest.g[1, :, z, x, pl.ds(32, 16), :] = small
     p_rest.start()
-    p_out.over_second()
-    p_in.over_first()
+
+    factor = 1.0 / math.sqrt(F * NTM * 8)
+    p_out.over_z(factor)
 
     r_o = lax.broadcasted_iota(jnp.int32, (2 * F, NEXT16), 0)
     c_o = lax.broadcasted_iota(jnp.int32, (2 * F, NEXT16), 1)
@@ -559,36 +621,19 @@
     o_input[...] += dot_nt(here_odd, conv_w[2])
     o_input[...] += dot_nt(ahead, conv_w[0])
 
-    factor = 1.0 / math.sqrt(F * NTM * 8)
     p_rest.over_core()
-    p_out.over_z(factor)
     p_in.over_second()
+    p_rest.pass_on()
+    p_in.over_z(factor)
     p_rest.over_first()
-    p_in.over_z(factor)
+    p_out.gathered()
+    o_fin_out[...] = p_out.fin[...]
     p_rest.over_second()
-    p_out.gathered()
-    for b in range(8):
-        o_out[:, 128 * b : 128 * b + 128] = p_out.fin[b].astype(F32)
+    p_in.gathered()
+    o_fin_in[...] = p_in.fin[...]
     p_rest.over_z(factor)
-    p_in.gathered()
-    for b in range(8):
-        for s in range(2):
-            o_in[:, 256 * b + 128 * s : 256 * b + 128 * s + 128] = p_in.fin[
-                b, pl.ds(32 * s, 32)
-            ].astype(F32)
     p_rest.gathered()
-    for b in range(8):
-        o_proj[:, 128 * b : 128 * b + 128] = p_rest.fin[b, pl.ds(0, 16)].astype(F32)
-    for y in range(NY):
-        cols = pl.ds(128 * y, 128)
-        o_conv[0, :, cols] = p_rest.fin[y, pl.ds(16, 16)].astype(F32)
-        o_conv[1, :, cols] = p_rest.fin[y, pl.ds(32, 16)].astype(F32)
-        o_conv[2, :, cols] = p_rest.fin[NY + y, pl.ds(16, 16)].astype(F32)
-        small = p_rest.fin[NY + y, pl.ds(32, 16)].astype(F32)[0:8]
-        mine = jnp.zeros((8, 32), F32)
-        for x in range(NX):
-            mine = mine + jnp.where(at.x == x, small[:, 32 * x : 32 * x + 32], 0.0)
-        o_misc[pl.ds(8 * y, 8), :] = mine
+    o_fin_rest[...] = p_rest.fin[...]
 
     loop(NTM - 1, lambda d: routed(d + 1).wait_send())
     for one in halos + [edge_up] + edges:
@@ -597,10 +642,40 @@
         part.close()
 
 
+def spread(
+    rows, f_out, f_in, f_rest, o_input, o_conv, o_proj, o_in, o_depth, o_gain, o_out, done
+):
+    whole = pltpu.make_async_copy(rows, o_input, done)
+    whole.start()
+    for b in range(8):
+        cols = pl.ds(128 * b, 128)
+        o_out[:, cols] = f_out[b].astype(F32)
+        o_proj[:, cols] = f_rest[b, pl.ds(0, 16)].astype(F32)
+        for s in range(2):
+            o_in[:, pl.ds(256 * b + 128 * s, 128)] = f_in[b, pl.ds(32 * s, 32)].astype(F32)
+    x = lax.rem(lax.axis_index("tm"), NX)
+    for y in range(NY):
+        cols = pl.ds(128 * y, 128)
+        o_conv[0, :, cols] = f_rest[y, pl.ds(16, 16)].astype(F32)
+        o_conv[1, :, cols] = f_rest[y, pl.ds(32, 16)].astype(F32)
+        o_conv[2, :, cols] = f_rest[NY + y, pl.ds(16, 16)].astype(F32)
+        small = f_rest[NY + y, pl.ds(32, 16)].astype(F32)[0:8]
+        mine = jnp.zeros((8, 32), F32)
+        for other in range(NX):
+            mine = mine + jnp.where(x == other, small[:, 32 * other : 32 * other + 32], 0.0)
+        if y < NY - 1:
+            o_depth[pl.ds(8 * y, 8), :] = mine
+        else:
+            o_depth[pl.ds(8 * y, 7), :] = mine[0:7]
+            o_gain[...] = mine[7:8]
+    whole.wait()
+
+
 def per_device(
     grad_attn, route, lengths, conv_pre, conv_in, conv_w, proj_w, in_w, depth_w, depth_gain, out_w
 ):
     vmem = pl.BlockSpec(memory_space=pltpu.VMEM)
+    anywhere = pl.BlockSpec(memory_space=pl.ANY)
     smem = pl.BlockSpec(memory_space=pltpu.SMEM)
     scratch = [
         pltpu.VMEM((NTM * CAP, D + IDX), BF),
@@ -630,8 +705,15 @@
         pltpu.VMEM((D, F), BF),
         pltpu.VMEM((CF, F), BF),
         pltpu.VMEM((F, NTM * CAP), BF),
-        pltpu.VMEM((CF, F), BF),
+        pltpu.VMEM((3, CF, F), BF),
         pltpu.VMEM((4, 16, D), F32),
+        pltpu.VMEM((8, EXT, 128), F32),
+        pltpu.VMEM((2 * F, CF), BF),
+        pltpu.VMEM((3, CF, CF), BF),
+        pltpu.VMEM((CF, D), BF),
+        pltpu.VMEM((D, 2 * D), BF),
+        pltpu.VMEM((D, D), BF),
+        pltpu.SemaphoreType.DMA((6,)),
         pltpu.SemaphoreType.DMA((NTM,)),
         pltpu.SemaphoreType.DMA((NTM,)),
         pltpu.SemaphoreType.DMA((6,)),
@@ -641,26 +723,34 @@
         scratch += part_scratch(rows)
     outs = pl.pallas_call(
         kernel,
-        out_shape=[
-            jax.ShapeDtypeStruct((2 * F, CF), F32),
-            jax.ShapeDtypeStruct((3, 16, CF), F32),
-            jax.ShapeDtypeStruct((16, D), F32),
-            jax.ShapeDtypeStruct((32, 2 * D), F32),
-            jax.ShapeDtypeStruct((32, 32), F32),
-            jax.ShapeDtypeStruct((32, D), F32),
-        ],
-        in_specs=[smem] + [vmem] * 10,
-        out_specs=[vmem] * 6,
+        out_shape=[jax.ShapeDtypeStruct((2 * F, CF), F32)]
+        + [jax.ShapeDtypeStruct((8, rows, 128), BF) for rows in PART_ROWS],
+        in_specs=[smem] + [vmem] * 2 + [anywhere] * 5 + [vmem] * 2 + [anywhere],
+        out_specs=[vmem] * 4,
         scratch_shapes=scratch,
         compiler_params=pltpu.CompilerParams(
             collective_id=0, has_side_effects=True, vmem_limit_bytes=62 * 2**20
         ),
     )(
         lengths, route, grad_attn[0], conv_pre[0], conv_in[0], conv_w, proj_w, in_w, depth_w,
-        depth_gain[None], out_w,
+        depth_gain, out_w,
     )
-    o_input, o_conv, o_proj, o_in, o_misc, o_out = outs
-    return (o_input[None], o_conv, o_proj, o_in, o_misc[:KW], o_misc[KW], o_out)
+    o_input, o_conv, o_proj, o_in, o_depth, o_gain, o_out = pl.pallas_call(
+        spread,
+        out_shape=[
+            jax.ShapeDtypeStruct((2 * F, CF), F32),
+            jax.ShapeDtypeStruct((3, 16, CF), F32),
+            jax.ShapeDtypeStruct((16, D), F32),
+            jax.ShapeDtypeStruct((32, 2 * D), F32),
+            jax.ShapeDtypeStruct((KW, 32), F32),
+            jax.ShapeDtypeStruct((1, 32), F32),
+            jax.ShapeDtypeStruct((32, D), F32),
+        ],
+        in_specs=[vmem] * 4,
+        out_specs=[anywhere] + [vmem] * 6,
+        scratch_shapes=[pltpu.SemaphoreType.DMA],
+    )(*outs)
+    return (o_input[None], o_conv, o_proj, o_in, o_depth, o_gain[0], o_out)
 
 
 def solution(mesh):

time: 132 us -> 108 us (0.82)
  Pallas kernels: 124 us -> 107 us
  local copies, waits for them, and re-layouts: 8.03 us -> 0 us
    pallas_call x1 -> x2, Pallas kernels: 124 us -> 107 us  [the longest x1 104 us: per_device(): pl.pallas_call(kernel, out_shape=[jax.ShapeDtypeStruct((2 * F, CF), F32)]...]
    unnamed x16 -> x0, local copies, waits for them, and re-layouts: 5.52 us -> none
where the time goes in v2:
time: 108 us
  Pallas kernels  107 us (99%)
    pallas_call x1, Pallas kernels, per_device(): pl.pallas_call(kernel, out_shape=[jax.ShapeDtypeStruct((2 * F, CF), F32)]...  104 us
    pallas_call x1, Pallas kernels, per_device(): pl.pallas_call(spread, out_shape=[jax.ShapeDtypeStruct((2 * F, CF), F32),...  3.07 us

profile of v2, /device:TPU:1, one launch (start us, length us, event | category | flops | bytes accessed | tf_op | source)
XLA Modules:
  0.0 107.5 jit_solution(12798818154327151276)
XLA Ops:
  0.6 103.8 %shard_map.162 = (f32[512,512]{1,0:T(8,128)}, bf16[8,32,128]{2,1,0:T(8,128)(2,1)}, bf16[8,64,128]{2,1,0:T(8,128)(2,1)}, bf16[8,48,128]{2,1,0:T(8,128)(2,1)}) custom-call(s32[1,4]{1,0:T(1,128)} %lengths.1, s32[1,256]{1,0:T(1,128)} %route.1, bf16[256,1024]{1,0:T(8,128)(2,1)} %bitcast.5, bf16[256,512]{1,0:T(8,128)(2,1)} %bitcast.7, bf16[512,512]{1,0:T(8,128)(2,1)} %bitcast.6, ...), custom_call_target="tpu_custom_call" | custom-call | tf_op jit(solution)/shard_map/pallas_call | solution.py:724
  104.5 3.1 %shard_map.163 = (f32[512,512]{1,0:T(8,128)}, f32[3,16,512]{2,1,0:T(8,128)}, f32[16,1024]{1,0:T(8,128)}, f32[32,2048]{1,0:T(8,128)}, f32[31,32]{1,0:T(8,128)}, /*index=5*/f32[1,32]{1,0:T(1,128)}, f32[32,1024]{1,0:T(8,128)}) custom-call(f32[512,512]{1,0:T(8,128)} %get-tuple-element.18.rows, bf16[8,32,128]{2,1,0:T(8,128)(2,1)} %get-tuple-element.19.f_out, ...), custom_call_target="tpu_custom_call" | custom-call | tf_op jit(solution)/shard_map/pallas_call | solution.py:738

commit v3 on v2

--- a/solution.py
+++ b/solution.py
@@ -198,7 +198,7 @@
         c = self.at.c
 
         def add(y):
-            self.g[c, y] = (self.g[c, y].astype(F32) + self.r0[y].astype(F32)).astype(BF)
+            self.g[c, y] = self.g[c, y] + self.r0[y]
 
         loop(NY, add)
         self.go(self.s1_pass() + self.s1_direct())
@@ -207,9 +207,9 @@
         self.arrived(self.s1_pass())
         for h, d in ((0, 1), (1, 3)):
             rows = self.rows_y(d, h)
-            rows[...] = (rows[...].astype(F32) + self.r1p[0, h].astype(F32)).astype(BF)
+            rows[...] = rows[...] + self.r1p[0, h]
             rows = self.rows_x(d, h)
-            rows[...] = (rows[...].astype(F32) + self.r1q[0, h].astype(F32)).astype(BF)
+            rows[...] = rows[...] + self.r1q[0, h]
         self.go(self.s1_on())
 
     def over_first(self):
@@ -221,7 +221,7 @@
             self.a1q[:, pl.ds(2 * h, 2)] = (total + self.r1q[2, h].astype(F32)).astype(BF)
         self.go(self.s2())
 
-    def over_second(self):
+    def over_second(self, join=None):
         self.arrived(self.s2())
         y, x = self.at.y, self.at.x
 
@@ -235,6 +235,8 @@
             self.a2[4 + i] = other.astype(BF)
 
         loop(4, add)
+        if join is not None:
+            join(self.a2)
         self.go(self.s3())
 
     def over_z(self, factor):
@@ -251,6 +253,60 @@
     def close(self):
         for one in self.sent:
             one.wait_send()
+
+
+class Small(Part):
+    def __init__(self, at, refs):
+        self.at = at
+        self.own, self.core, self.from_y, self.some, self.from_x, self.send, self.recv = refs
+        self.sent = []
+
+    def over_y(self):
+        return [
+            self.copy(
+                d, self.own.at[lax.rem(self.at.y + d, NY)], self.from_y.at[d - 1], self.at.at_y(d)
+            )
+            for d in range(1, 4)
+        ]
+
+    def over_x(self):
+        return [
+            self.copy(3 + d, self.some, self.from_x.at[d - 1], self.at.at_x(d)) for d in range(1, 4)
+        ]
+
+    def s0(self):
+        return [self.copy(0, self.own, self.core, self.at.at_c())]
+
+    def begin(self, terms):
+        self.own[...] = terms[...].astype(BF)
+        self.go(self.s0())
+
+    def second(self):
+        self.arrived(self.s0())
+        for one in self.s0():
+            one.wait_send()
+        self.sent = []
+        self.own[...] = self.own[...] + self.core[...]
+        self.go(self.over_y())
+
+    def total(self, first, others):
+        total = first.astype(F32)
+        for d in range(3):
+            total = total + others[d].astype(F32)
+        return total.astype(BF)
+
+    def third(self):
+        self.arrived(self.over_y())
+        self.some[...] = self.total(self.own[self.at.y], self.from_y)
+        self.go(self.over_x())
+
+    def join(self, sums):
+        self.arrived(self.over_x())
+        total = self.total(self.some[...], self.from_x).astype(F32)
+        for z in range(NZ):
+            there = sums[z, pl.ds(32, 16)].astype(F32)
+            mine = total[:, 128 * z : 128 * z + 128]
+            sums[z, pl.ds(32, 16)] = jnp.where(self.at.c == 1, mine, there).astype(BF)
 
 
 def kernel(
@@ -266,6 +322,7 @@
     at = Place()
     tm = at.tm
     p_out, p_in, p_rest = (Part(at, parts_refs[13 * i : 13 * i + 13]) for i in range(3))
+    p_small = Small(at, parts_refs[39:])
     left, right = (at.dp, lax.rem(tm + NTM - 1, NTM)), (at.dp, lax.rem(tm + 1, NTM))
 
     loads = [
@@ -355,6 +412,9 @@
     glu[pl.ds(EXT, 8), :] = jnp.zeros((8, D), F32)
     dmix[pl.ds(EXT, 8), :] = jnp.zeros((8, D), F32)
     dj[pl.ds(F, 16), :] = jnp.zeros((16, 2 * D), BF)
+    dgs[:, pl.ds(8, 8), :] = jnp.zeros((4, 8, D), F32)
+    for y in range(NY):
+        p_rest.g[1, y, :, :, pl.ds(32, 16), :] = jnp.zeros((NZ, NX, 16, 128), BF)
 
     for one in loads[2:4]:
         one.wait()
@@ -497,6 +557,20 @@
     out_terms(1 - at.c)
     p_out.start()
     out_terms(at.c)
+
+    def depth(j):
+        cols = block(j, 128)
+        shift_all(shifts, glu, cols)
+        total = [None] * KW
+        for r in range(0, F, 64):
+            grad = dmix[pl.ds(H + r, 64), cols]
+            for k in range(KW):
+                rows = shifted(shifts, k, r, 64)
+                term = jnp.sum((rows * linked[k, pl.ds(r, 64)] * grad).reshape(8, 8, 128), axis=0)
+                total[k] = term if r == 0 else total[k] + term
+        for k in range(KW):
+            dgs[k // 8, pl.ds(k % 8, 1), cols] = jnp.sum(total[k], axis=0, keepdims=True)
+
     p_out.over_core()
 
     for one in edges:
@@ -580,34 +654,19 @@
 
     rest_terms(0)
     rest_terms(1)
-    p_in.pass_on()
     for tap, core, row in ((0, 0, 16), (1, 0, 32), (2, 1, 16)):
         conv_terms(tap, core, row)
+    p_rest.start()
     p_out.over_second()
-
-    def depth(j):
-        cols = block(j, 128)
-        shift_all(shifts, glu, cols)
-        total = [None] * KW
-        for r in range(0, F, 64):
-            grad = dmix[pl.ds(H + r, 64), cols]
-            for k in range(KW):
-                rows = shifted(shifts, k, r, 64)
-                term = jnp.sum((rows * linked[k, pl.ds(r, 64)] * grad).reshape(8, 8, 128), axis=0)
-                total[k] = term if r == 0 else total[k] + term
-        for k in range(KW):
-            dgs[k // 8, pl.ds(k % 8, 1), cols] = jnp.sum(total[k], axis=0, keepdims=True)
-
-    dgs[:, pl.ds(8, 8), :] = jnp.zeros((4, 8, D), F32)
-    loop(8, depth)
+    loop(2, depth)
+    p_in.pass_on()
+    p_rest.over_core()
+    loop(3, lambda j: depth(2 + j))
+    p_in.over_first()
+    p_rest.pass_on()
+    loop(3, lambda j: depth(5 + j))
     dgs[3, pl.ds(7, 1), :] = jnp.sum(gainsum[...], axis=0, keepdims=True)
-    p_in.over_first()
-    for z in range(NZ):
-        small = dgs[:, :, 128 * z : 128 * z + 128].astype(BF)
-        for x in range(NX):
-            p_rest.g[1, :, z, x, pl.ds(32, 16), :] = small
-    p_rest.start()
-
+    p_small.begin(dgs)
     factor = 1.0 / math.sqrt(F * NTM * 8)
     p_out.over_z(factor)
 
@@ -621,14 +680,14 @@
     o_input[...] += dot_nt(here_odd, conv_w[2])
     o_input[...] += dot_nt(ahead, conv_w[0])
 
-    p_rest.over_core()
+    p_small.second()
     p_in.over_second()
-    p_rest.pass_on()
+    p_rest.over_first()
+    p_small.third()
     p_in.over_z(factor)
-    p_rest.over_first()
+    p_rest.over_second(p_small.join)
     p_out.gathered()
     o_fin_out[...] = p_out.fin[...]
-    p_rest.over_second()
     p_in.gathered()
     o_fin_in[...] = p_in.fin[...]
     p_rest.over_z(factor)
@@ -638,7 +697,7 @@
     loop(NTM - 1, lambda d: routed(d + 1).wait_send())
     for one in halos + [edge_up] + edges:
         one.wait_send()
-    for part in (p_out, p_in, p_rest):
+    for part in (p_out, p_in, p_rest, p_small):
         part.close()
 
 
@@ -721,6 +780,15 @@
     ]
     for rows in PART_ROWS:
         scratch += part_scratch(rows)
+    scratch += [
+        pltpu.VMEM((NY, 16, D), BF),
+        pltpu.VMEM((NY, 16, D), BF),
+        pltpu.VMEM((3, 16, D), BF),
+        pltpu.VMEM((16, D), BF),
+        pltpu.VMEM((3, 16, D), BF),
+        pltpu.SemaphoreType.DMA((7,)),
+        pltpu.SemaphoreType.DMA((7,)),
+    ]
     outs = pl.pallas_call(
         kernel,
         out_shape=[jax.ShapeDtypeStruct((2 * F, CF), F32)]

time: 108 us -> 105 us (0.972)
  Pallas kernels: 107 us -> 104 us
    pallas_call x1, Pallas kernels: 104 us -> 101 us  [per_device(): pl.pallas_call(kernel, out_shape=[jax.ShapeDtypeStruct((2 * F, CF), F32)]...]
where the time goes in v3:
time: 105 us
  Pallas kernels  104 us (99%)
    pallas_call x1, Pallas kernels, per_device(): pl.pallas_call(kernel, out_shape=[jax.ShapeDtypeStruct((2 * F, CF), F32)]...  101 us
    pallas_call x1, Pallas kernels, per_device(): pl.pallas_call(spread, out_shape=[jax.ShapeDtypeStruct((2 * F, CF), F32),...  3.07 us

profile of v3, /device:TPU:1, one launch (start us, length us, event | category | flops | bytes accessed | tf_op | source)
XLA Modules:
  0.0 104.6 jit_solution(956344608205351090)
XLA Ops:
  0.6 100.9 %shard_map.162 = (f32[512,512]{1,0:T(8,128)}, bf16[8,32,128]{2,1,0:T(8,128)(2,1)}, bf16[8,64,128]{2,1,0:T(8,128)(2,1)}, bf16[8,48,128]{2,1,0:T(8,128)(2,1)}) custom-call(s32[1,4]{1,0:T(1,128)} %lengths.1, s32[1,256]{1,0:T(1,128)} %route.1, bf16[256,1024]{1,0:T(8,128)(2,1)} %bitcast.5, bf16[256,512]{1,0:T(8,128)(2,1)} %bitcast.7, bf16[512,512]{1,0:T(8,128)(2,1)} %bitcast.6, ...), custom_call_target="tpu_custom_call" | custom-call | tf_op jit(solution)/shard_map/pallas_call | solution.py:792
  101.5 3.1 %shard_map.163 = (f32[512,512]{1,0:T(8,128)}, f32[3,16,512]{2,1,0:T(8,128)}, f32[16,1024]{1,0:T(8,128)}, f32[32,2048]{1,0:T(8,128)}, f32[31,32]{1,0:T(8,128)}, /*index=5*/f32[1,32]{1,0:T(1,128)}, f32[32,1024]{1,0:T(8,128)}) custom-call(f32[512,512]{1,0:T(8,128)} %get-tuple-element.18.rows, bf16[8,32,128]{2,1,0:T(8,128)(2,1)} %get-tuple-element.19.f_out, ...), custom_call_target="tpu_custom_call" | custom-call | tf_op jit(solution)/shard_map/pallas_call | solution.py:806

commit v4 on v3

--- a/solution.py
+++ b/solution.py
@@ -395,7 +395,11 @@
             (at.dp, other),
         )
 
-    loop(NTM - 1, lambda d: routed(d + 1).start())
+    def both_ways(i):
+        near = lax.div(i, 2) + 1
+        routed(jnp.where(lax.rem(i, 2) == 0, near, NTM - near)).start()
+
+    loop(NTM - 1, both_ways)
     incoming[block(tm, CAP)] = outgoing[block(tm, CAP)]
 
     bound0 = lengths[0, 0]

time: 105 us -> 104 us (level)
  no operation moved by 1% of the time
where the time goes in v4:
time: 104 us
  Pallas kernels  103 us (99%)
    pallas_call x1, Pallas kernels, per_device(): pl.pallas_call(kernel, out_shape=[jax.ShapeDtypeStruct((2 * F, CF), F32)]...  99.9 us
    pallas_call x1, Pallas kernels, per_device(): pl.pallas_call(spread, out_shape=[jax.ShapeDtypeStruct((2 * F, CF), F32),...  3.07 us

profile of v4, /device:TPU:1, one launch (start us, length us, event | category | flops | bytes accessed | tf_op | source)
XLA Modules:
  0.0 103.7 jit_solution(4544212348871572978)
XLA Ops:
  0.6 99.9 %shard_map.162 = (f32[512,512]{1,0:T(8,128)}, bf16[8,32,128]{2,1,0:T(8,128)(2,1)}, bf16[8,64,128]{2,1,0:T(8,128)(2,1)}, bf16[8,48,128]{2,1,0:T(8,128)(2,1)}) custom-call(s32[1,4]{1,0:T(1,128)} %lengths.1, s32[1,256]{1,0:T(1,128)} %route.1, bf16[256,1024]{1,0:T(8,128)(2,1)} %bitcast.5, bf16[256,512]{1,0:T(8,128)(2,1)} %bitcast.7, bf16[512,512]{1,0:T(8,128)(2,1)} %bitcast.6, ...), custom_call_target="tpu_custom_call" | custom-call | tf_op jit(solution)/shard_map/pallas_call | solution.py:796
  100.6 3.1 %shard_map.163 = (f32[512,512]{1,0:T(8,128)}, f32[3,16,512]{2,1,0:T(8,128)}, f32[16,1024]{1,0:T(8,128)}, f32[32,2048]{1,0:T(8,128)}, f32[31,32]{1,0:T(8,128)}, /*index=5*/f32[1,32]{1,0:T(1,128)}, f32[32,1024]{1,0:T(8,128)}) custom-call(f32[512,512]{1,0:T(8,128)} %get-tuple-element.18.rows, bf16[8,32,128]{2,1,0:T(8,128)(2,1)} %get-tuple-element.19.f_out, ...), custom_call_target="tpu_custom_call" | custom-call | tf_op jit(solution)/shard_map/pallas_call | solution.py:810
